TPU v7x, 32 devices: a whole 2x2x4 slice. The times are simulated.
32 devices in a mesh: groups: 2 (over y), wide: 16 (over z, x, core).
Axes of the slice: x: 2, y: 2, z: 4, core: 2. Of those that a mesh axis runs over, the one named last changes fastest.
Arguments:
- density: bfloat16 [4096, 2048], P(('groups', 'wide')), parts along dimension 0, may hold values from -0.0234375 to 0.0234375
- ao_values: bfloat16 [2048, 2, 32, 128], P(('groups', 'wide')), parts along dimension 0, may hold values from -6 to 6
- block_lists: int32 [2048, 2], P(('groups', 'wide')), parts along dimension 0, may hold values from 0 to 15, all different within a row; in each aligned block of 64 rows (0 to 63, 64 to 127, ...) at most 8 rows name the same one
- counts: int32 [2048], P(('groups', 'wide')), parts along dimension 0, may hold values from 1 to 2
- other_features: float32 [2048, 10, 32], P(('groups', 'wide')), parts along dimension 0, may hold values from -6 to 6
- quad_weights: float32 [2048, 32], P(('groups', 'wide')), parts along dimension 0, may hold values from 0.02 to 0.2
- w_in: float32 [11, 256], replicated, may hold values from -1.75 to 1.75
- biases: float32 [4, 256], replicated, may hold values from -2.5 to 2.5
- w_layers: bfloat16 [3, 256, 256], replicated, may hold values from -0.375 to 0.375
- w_out: float32 [256], replicated, may hold values from -0.375 to 0.375
Outputs:
- potential: bfloat16 [4096, 2048], P(('groups', 'wide')), parts along dimension 0
- weight_grads: float32 [6, 256, 256], P('groups'), parts along dimension 0
- input_grads: float32 [22, 256], P('groups'), parts along dimension 0
- bias_grads: float32 [8, 256], P('groups'), parts along dimension 0
- output_grads: float32 [512], P('groups'), parts along dimension 0
There are 2 independent parts, one for each index of `groups`. A program takes and returns all parts, laid end to end along the dimension named above; an argument that names none is the same for every part. Nothing has to cross between parts.
Inputs may be any that keep to these rules, and one draw needn't show every extreme that they name: `block_lists`: the 2 entries of a batch are different blocks; among the 64 batches of one index of wide no block is named by more than 8 of them.
All inputs are finite; a program needn't handle non-finite values.
Results may differ from a plain program's by a relative error of at most 0.0035.
Values may be sent and summed in bfloat16 or wider, within the bound.
A program may use at most 128 MiB of HBM per device.

v0:
```python
import jax
import jax.numpy as jnp
from jax import lax
from jax.sharding import PartitionSpec as P

highest = lax.Precision.HIGHEST


def owner_parts(ao_slots, block_ids, blocks, list_len):
    row_pick = block_ids[:, :, list_len]
    row_block = jnp.take_along_axis(ao_slots, row_pick[:, :, None, None, None], axis=2)[:, :, 0]
    accum_total = jnp.zeros(row_block.shape[:3], jnp.float32)
    for entry_pos in range(list_len):
        chosen = blocks[block_ids[:, :, entry_pos]]
        product = jnp.einsum(
            "ncpm,ncmq->ncpq", row_block, chosen, preferred_element_type=jnp.float32
        )
        accum_total = accum_total + jnp.sum(
            product * ao_slots[:, :, entry_pos].astype(jnp.float32), axis=3
        )
    return accum_total


def shards(
    density,
    ao_values,
    block_lists,
    counts,
    other_features,
    quad_weights,
    w_in,
    biases,
    w_layers,
    w_out,
):
    dev_count = lax.axis_size("wide")
    batch_count, list_len, point_count, block_width = ao_values.shape
    block_count = density.shape[1] // block_width
    slot_cap = max(2, (batch_count * list_len + block_count - 1) // block_count)
    slot_count = dev_count * slot_cap
    hidden_width = w_out.shape[0]
    layer_count = w_layers.shape[0]
    live_mask = jnp.arange(list_len)[None, :] < counts[:, None]
    masked = jnp.where(live_mask[:, :, None, None], ao_values, jnp.zeros((), ao_values.dtype))
    target = block_lists.reshape(-1)
    alive_flat = live_mask.reshape(-1)
    entry_ids = jnp.arange(target.shape[0], dtype=jnp.int32)
    earlier = (
        (target[:, None] == target[None, :])
        & alive_flat[None, :]
        & (entry_ids[None, :] < entry_ids[:, None])
    )
    slot_rank = jnp.sum(earlier.astype(jnp.int32), axis=1)
    slot_of = target * slot_cap + slot_rank
    slot_table = (
        slot_of[None, :] == jnp.arange(slot_count, dtype=jnp.int32)[:, None]
    ) & alive_flat[None, :]
    filled = jnp.any(slot_table, axis=1)
    source = jnp.sum(jnp.where(slot_table, entry_ids[None, :], 0), axis=1)
    src_batch = source // list_len
    src_entry = source % list_len
    send_ao = jnp.where(filled[:, None, None, None], masked[src_batch], jnp.zeros((), masked.dtype))
    send_ids = jnp.concatenate([block_lists[src_batch], src_entry[:, None]], axis=1)
    send_ao = send_ao.reshape(dev_count, slot_cap, list_len, point_count, block_width)
    send_ids = send_ids.reshape(dev_count, slot_cap, list_len + 1)
    blocks = density.reshape(block_width, block_count, block_width).transpose(1, 0, 2)
    recv_ao, recv_ids = (
        lax.all_to_all(send_ao, "wide", split_axis=0, concat_axis=0, tiled=True),
        lax.all_to_all(send_ids, "wide", split_axis=0, concat_axis=0, tiled=True),
    )
    partial_value = owner_parts(recv_ao, recv_ids, blocks, list_len)
    returned = lax.all_to_all(partial_value, "wide", split_axis=0, concat_axis=0, tiled=True)
    batch_pick = (
        (src_batch[:, None] == jnp.arange(batch_count, dtype=jnp.int32)[None, :]) & filled[:, None]
    ).astype(jnp.float32)
    density_pts = jnp.dot(
        batch_pick.T, returned.reshape(slot_count, point_count), precision=highest
    )
    features = jnp.concatenate([density_pts[:, None, :], other_features], axis=1)
    pre_act = jnp.einsum("bfp,fh->bph", features, w_in, precision=highest) + biases[0]
    row_count = batch_count * point_count
    activations = [jnp.tanh(pre_act).reshape(row_count, hidden_width).astype(jnp.bfloat16)]
    for layer_idx in range(layer_count):
        inner_sum = (
            jnp.dot(activations[-1], w_layers[layer_idx], preferred_element_type=jnp.float32)
            + biases[layer_idx + 1]
        )
        activations.append(jnp.tanh(inner_sum).astype(jnp.bfloat16))
    top_act = activations[-1].astype(jnp.float32)
    out_score = jnp.dot(top_act, w_out, precision=highest)
    enhance = 2.0 * jax.nn.sigmoid(out_score)
    rho_flat = density_pts.reshape(row_count)
    weight_flat = quad_weights.reshape(row_count)
    grad_score = weight_flat * rho_flat * enhance * (1.0 - 0.5 * enhance)
    out_grad = jnp.dot(grad_score, top_act, precision=highest)
    grad_act = grad_score[:, None] * w_out[None, :]
    layer_grads = [None] * layer_count
    bias_list = [None] * (layer_count + 1)
    for layer_idx in reversed(range(layer_count)):
        act_after = activations[layer_idx + 1].astype(jnp.float32)
        grad_pre = grad_act * (1.0 - act_after * act_after)
        grad_round = grad_pre.astype(jnp.bfloat16)
        weight_term = jnp.dot(
            activations[layer_idx].T, grad_round, preferred_element_type=jnp.float32
        )
        weight_term = lax.psum(weight_term, "wide")
        layer_grads[layer_idx] = weight_term
        bias_list[layer_idx + 1] = jnp.sum(grad_pre, axis=0)
        grad_act = jnp.dot(grad_round, w_layers[layer_idx].T, preferred_element_type=jnp.float32)
    act_first = activations[0].astype(jnp.float32)
    grad_first = grad_act * (1.0 - act_first * act_first)
    bias_list[0] = jnp.sum(grad_first, axis=0)
    feature_rows = features.transpose(0, 2, 1).reshape(row_count, features.shape[1])
    input_term = jnp.dot(feature_rows.T, grad_first, precision=highest)
    bias_term = jnp.stack(bias_list)
    grad_rho = jnp.dot(grad_first, w_in[0], precision=highest)
    potential_weight = (weight_flat * enhance + grad_rho).reshape(batch_count, point_count)
    send_weight = jnp.where(filled[:, None], potential_weight[src_batch], 0.0).reshape(
        dev_count, slot_cap, point_count
    )
    recv_weight = lax.all_to_all(send_weight, "wide", split_axis=0, concat_axis=0, tiled=True)
    weight_grads = jnp.stack(layer_grads)
    input_grads, bias_grads, output_grads = lax.psum((input_term, bias_term, out_grad), "wide")
    row_pick = recv_ids[:, :, list_len]
    row_block = jnp.take_along_axis(recv_ao, row_pick[:, :, None, None, None], axis=2)[:, :, 0]
    weighted = (row_block.astype(jnp.float32) * recv_weight[:, :, :, None]).astype(jnp.bfloat16)
    accum_total = jnp.zeros((block_count, block_width, block_width), jnp.float32)
    for entry_pos in range(list_len):
        contrib = jnp.einsum(
            "ncpm,ncpq->ncmq",
            weighted,
            recv_ao[:, :, entry_pos],
            preferred_element_type=jnp.float32,
        )
        accum_total = accum_total + jax.ops.segment_sum(
            contrib.reshape(slot_count, block_width, block_width),
            recv_ids[:, :, entry_pos].reshape(slot_count),
            num_segments=block_count,
        )
    potential = (
        accum_total.transpose(1, 0, 2)
        .reshape(block_width, block_count * block_width)
        .astype(jnp.bfloat16)
    )
    return (potential, weight_grads, input_grads, bias_grads, output_grads)


def solution(mesh):
    placed = (
        P(("groups", "wide"), None),
        P(("groups", "wide"), None, None, None),
        P(("groups", "wide"), None),
        P(("groups", "wide")),
        P(("groups", "wide"), None, None),
        P(("groups", "wide"), None),
        P(),
        P(),
        P(),
        P(),
    )
    return jax.shard_map(
        shards,
        mesh=mesh,
        in_specs=placed,
        out_specs=(
            P(("groups", "wide"), None),
            P("groups", None, None),
            P("groups", None),
            P("groups", None),
            P("groups"),
        ),
        check_vma=False,
    )
```

profile of v0, /device:TPU:0, one launch (start us, length us, event | category | flops | bytes accessed | tf_op | source)
XLA Modules:
  0.0 248.3 jit_solution(3030077430687878207)
XLA Ops:
  10.9 7.4 %all-to-all-start = ((s32[16,8,3]{1,2,0:T(4,128)}), s32[16,8,3]{1,2,0:T(4,128)S(1)}, u32[]{:S(2)}, u32[]{:S(2)}) async-start(s32[16,8,3]{1,2,0:T(4,128)} %pad_add_fusion), calls=%async_computation | async-start | bytes 65536 | tf_op jit(solution)/shard_map/all_to_all | solution.py:69
  18.3 1.4 broadcast_select_fusion.2
  21.1 1.9 copy.121
  23.0 1.9 all-to-all-done
  24.9 4.2 %all-to-all-start.1 = ((bf16[16,8,2,32,128]{4,3,1,2,0:T(8,128)(2,1)}), bf16[16,8,2,32,128]{4,3,1,2,0:T(8,128)(2,1)S(1)}, u32[]{:S(2)}, u32[]{:S(2)}) async-start(bf16[16,8,2,32,128]{4,3,1,2,0:T(8,128)(2,1)} %copy.121), calls=%async_computation.1 | async-start | bytes 4194304 | tf_op jit(solution)/shard_map/all_to_all | solution.py:68
  31.0 3.1 %gather_fusion.3 = bf16[128,128,128]{2,1,0:T(8,128)(2,1)} fusion(bf16[16,128,128]{2,1,0:T(8,128)(2,1)S(1)} %bitcast.149, s32[1024]{0:T(1024)S(1)} %pad_clamp_fusion), kind=kCustom, calls=%fused_computation.4 | custom fusion | bytes 8389120 | tf_op jit(solution)/shard_map/gather | solution.py:14
  34.1 3.0 %gather_fusion.2 = bf16[128,128,128]{2,1,0:T(8,128)(2,1)} fusion(bf16[16,128,128]{2,1,0:T(8,128)(2,1)S(1)} %bitcast.150, s32[1024]{0:T(1024)S(1)} %pad_clamp_fusion.1), kind=kCustom, calls=%fused_computation.3 | custom fusion | bytes 8389120 | tf_op jit(solution)/shard_map/gather | solution.py:14
  37.1 33.2 %all-to-all-done.1 = bf16[16,8,2,32,128]{4,3,1,2,0:T(8,128)(2,1)S(1)} async-done(((bf16[16,8,2,32,128]{4,3,1,2,0:T(8,128)(2,1)}), bf16[16,8,2,32,128]{4,3,1,2,0:T(8,128)(2,1)S(1)}, u32[]{:S(2)}, u32[]{:S(2)}) %all-to-all-start.1) | async-done | bytes 2097184 | tf_op jit(solution)/shard_map/all_to_all | solution.py:68
  70.2 1.1 gather_fusion.5
  71.3 3.7 %multiply_reduce_fusion = f32[16,8,32]{2,1,0:T(8,128)S(1)} fusion(bf16[16,8,128,128]{3,2,1,0:T(8,128)(2,1)} %bitcast.157, bf16[16,8,2,32,128]{4,3,1,2,0:T(8,128)(2,1)S(1)} %all-to-all-done.1, bf16[16,8,1,32,128]{4,3,1,0,2:T(8,128)(2,1)S(1)} %bitcast.153, pred[16,8]{1,0:T(8,128)(4,1)S(1)} %copy.120), kind=kOutput, calls=%fused_computation.25 | convolution fusion | flops 136310784 | bytes 6307968 | tf_op jit(solution)/shard_map/ncpm,ncmq->ncpq/dot_general | solution.py:15
  75.0 1.4 multiply_reduce_fusion.1
  77.1 11.2 %all-to-all-start.2 = ((f32[16,1,256]{2,1,0:T(1,128)}), f32[16,1,256]{2,1,0:T(1,128)S(1)}, u32[]{:S(2)}, u32[]{:S(2)}) async-start(f32[16,1,256]{2,1,0:T(1,128)} %reshape.339), calls=%async_computation.2 | async-start | bytes 32768 | tf_op jit(solution)/shard_map/all_to_all | solution.py:72
  89.8 5.0 %all-to-all-done.2 = f32[16,1,256]{2,1,0:T(1,128)S(1)} async-done(((f32[16,1,256]{2,1,0:T(1,128)}), f32[16,1,256]{2,1,0:T(1,128)S(1)}, u32[]{:S(2)}, u32[]{:S(2)}) %all-to-all-start.2) | async-done | bytes 16416 | tf_op jit(solution)/shard_map/all_to_all | solution.py:72
  98.4 3.0 %tanh_convert_fusion = bf16[64,32,256]{2,1,0:T(8,128)(2,1)S(1)} fusion(f32[64,11,32]{2,1,0:T(8,128)} %copy.129, f32[256]{0:T(256)} %bitcast.179, f32[11,256]{1,0:T(8,128)} %param.18), kind=kOutput, calls=%fused_computation.24 | convolution fusion | flops 70254592 | bytes 1150976 | tf_op jit(solution)/shard_map/bfp,fh->bph/dot_general | solution.py:80
  101.4 1.4 fusion.3
  105.7 1.4 fusion.65
  107.1 1.5 convolution_bitcast_fusion
  108.6 1.2 fusion.66
  109.8 2.5 fusion.67
  112.3 1.2 convolution_bitcast_fusion.2
  113.5 1.2 convolution_bitcast_fusion.1
  114.6 2.3 fusion.70
  116.9 1.1 copy.132
  118.9 3.6 %fusion.52 = f32[1,2048]{1,0:T(1,128)S(1)} fusion(f32[2048,256]{1,0:T(8,128)} %get-tuple-element.51, f32[11,256]{1,0:T(8,128)S(1)} %copy-done.6), kind=kOutput, calls=%fused_computation.114 | convolution fusion | flops 6291456 | bytes 2106368 | tf_op jit(solution)/shard_map/dot_general | solution.py:116
  122.5 1.8 fusion.69
  126.0 3.5 %all-to-all-start.3 = ((f32[16,1,256]{2,1,0:T(1,128)}), f32[16,1,256]{2,1,0:T(1,128)S(1)}, u32[]{:S(2)}, u32[]{:S(2)}) async-start(f32[16,1,256]{2,1,0:T(1,128)} %reshape.341), calls=%async_computation.3 | async-start | bytes 32768 | tf_op jit(solution)/shard_map/all_to_all | solution.py:121
  130.3 62.2 %all-reduce = (f32[11,256]{1,0:T(8,128)}, f32[4,256]{1,0:T(4,128)}, f32[256]{0:T(256)}) all-reduce(f32[11,256]{1,0:T(8,128)S(1)} %fusion.69, f32[4,256]{1,0:T(4,128)S(1)} %pad_maximum_fusion.2, f32[256]{0:T(256)S(1)} %bitcast.177), channel_id=1, replica_groups=mesh['groups'=2,'wide'=16] {'wide'}, use_global_device_ids=true, to_apply=%region_10.12 | all-reduce | flops 4096 | bytes 32768 | tf_op jit(solution)/shard_map/psum | solution.py:123
  193.3 5.2 %fusion.11 = f32[16,8,128,128]{3,2,1,0:T(8,128)} fusion(bf16[16,8,2,32,128]{4,3,1,2,0:T(8,128)(2,1)S(1)} %all-to-all-done.1, f32[16,8,32]{2,1,0:T(8,128)S(1)} %reshape.342, bf16[16,8,1,32,128]{4,3,1,0,2:T(8,128)(2,1)S(1)} %bitcast.155, pred[16,8]{1,0:T(8,128)(4,1)S(1)} %copy.120), kind=kOutput, calls=%fused_computation.39 | convolution fusion | flops 136314880 | bytes 10553344 | tf_op jit(solution)/shard_map/ncpm,ncpq->ncmq/dot_general | solution.py:129
  198.5 5.2 %fusion.10 = f32[16,8,128,128]{3,2,1,0:T(8,128)} fusion(bf16[16,8,2,32,128]{4,3,1,2,0:T(8,128)(2,1)S(1)} %all-to-all-done.1, f32[16,8,32]{2,1,0:T(8,128)S(1)} %reshape.342, bf16[16,8,1,32,128]{4,3,1,0,2:T(8,128)(2,1)S(1)} %bitcast.156, pred[16,8]{1,0:T(8,128)(4,1)S(1)} %copy.120), kind=kOutput, calls=%fused_computation.38 | convolution fusion | flops 136314880 | bytes 10553344 | tf_op jit(solution)/shard_map/ncpm,ncpq->ncmq/dot_general | solution.py:129
  203.8 17.0 %scatter_fusion.1 = f32[16,128,128]{2,1,0:T(8,128)S(1)} fusion(f32[16,128,128]{2,1,0:T(8,128)S(1)} %broadcast.211.clone.1, s32[128]{0:T(128)S(1)} %copy-done.15, f32[128,128,128]{2,1,0:T(8,128)} %bitcast.152), kind=kCustom, calls=%fused_computation.7 | custom fusion | flops 2097152 | bytes 25166336 | tf_op jit(solution)/shard_map/scatter-add | solution.py:135
  221.0 17.0 %scatter_fusion = f32[16,128,128]{2,1,0:T(8,128)S(1)} fusion(f32[16,128,128]{2,1,0:T(8,128)S(1)} %broadcast.211.clone, s32[128]{0:T(128)S(1)} %copy-done.14, f32[128,128,128]{2,1,0:T(8,128)} %bitcast.151), kind=kCustom, calls=%fused_computation.6 | custom fusion | flops 2097152 | bytes 25166336 | tf_op jit(solution)/shard_map/scatter-add | solution.py:135
  239.4 2.0 pad_maximum_fusion
  (116 shorter events, 21.0 us)
Async XLA Ops:
  9.4 11.4 %copy-start.8 = (s32[1024]{0:T(1024)}, s32[1024]{0:T(1024)S(1)}, u32[]{:S(2)}) copy-start(s32[1024]{0:T(1024)S(1)} %pad_clamp_fusion.2) | copy-start | bytes 12292
  10.9 14.0 %all-to-all-start = ((s32[16,8,3]{1,2,0:T(4,128)}), s32[16,8,3]{1,2,0:T(4,128)S(1)}, u32[]{:S(2)}, u32[]{:S(2)}) async-start(s32[16,8,3]{1,2,0:T(4,128)} %pad_add_fusion), calls=%async_computation | async-start | bytes 65536 | tf_op jit(solution)/shard_map/all_to_all | solution.py:69
  23.0 6.2 %copy-start.3 = (bf16[128,2048]{1,0:T(8,128)(2,1)S(1)}, bf16[128,2048]{1,0:T(8,128)(2,1)}, u32[]{:S(2)}) copy-start(bf16[128,2048]{1,0:T(8,128)(2,1)} %param.12) | copy-start | bytes 1572868
  24.9 45.3 %all-to-all-start.1 = ((bf16[16,8,2,32,128]{4,3,1,2,0:T(8,128)(2,1)}), bf16[16,8,2,32,128]{4,3,1,2,0:T(8,128)(2,1)S(1)}, u32[]{:S(2)}, u32[]{:S(2)}) async-start(bf16[16,8,2,32,128]{4,3,1,2,0:T(8,128)(2,1)} %copy.121), calls=%async_computation.1 | async-start | bytes 4194304 | tf_op jit(solution)/shard_map/all_to_all | solution.py:68
  29.1 0.7 copy-start.11
  71.3 3.7 %copy-start.1 = (bf16[128,128,128]{2,1,0:T(8,128)(2,1)S(1)}, bf16[128,128,128]{2,1,0:T(8,128)(2,1)}, u32[]{:S(2)}) copy-start(bf16[128,128,128]{2,1,0:T(8,128)(2,1)} %gather_fusion.2) | copy-start | bytes 12582916
  75.0 13.4 %copy-start.7 = (f32[64,32]{0,1:T(8,128)S(1)}, f32[64,32]{0,1:T(8,128)}, u32[]{:S(2)}) copy-start(f32[64,32]{0,1:T(8,128)} %param.17) | copy-start | bytes 24580
  75.0 21.5 %copy-start.4 = (f32[64,10,32]{0,2,1:T(8,128)S(1)}, f32[64,10,32]{0,2,1:T(8,128)}, u32[]{:S(2)}) copy-start(f32[64,10,32]{0,2,1:T(8,128)} %param.16) | copy-start | bytes 245764
  77.1 17.7 %all-to-all-start.2 = ((f32[16,1,256]{2,1,0:T(1,128)}), f32[16,1,256]{2,1,0:T(1,128)S(1)}, u32[]{:S(2)}, u32[]{:S(2)}) async-start(f32[16,1,256]{2,1,0:T(1,128)} %reshape.339), calls=%async_computation.2 | async-start | bytes 32768 | tf_op jit(solution)/shard_map/all_to_all | solution.py:72
  98.4 4.4 %copy-start.5 = (bf16[3,256,256]{2,1,0:T(8,128)(2,1)S(1)}, bf16[3,256,256]{2,1,0:T(8,128)(2,1)}, u32[]{:S(2)}) copy-start(bf16[3,256,256]{2,1,0:T(8,128)(2,1)} %param.20) | copy-start | bytes 1179652
  98.4 4.4 %copy-start.17 = (f32[1,256]{1,0:T(1,128)S(1)}, f32[1,256]{1,0:T(1,128)}, u32[]{:S(2)}) copy-start(f32[1,256]{1,0:T(1,128)} %get-tuple-element.45) | copy-start | bytes 3076
  101.4 1.9 copy-start.16
  102.8 0.9 copy-start.12
  103.7 3.4 %copy-start.2 = (bf16[2048,256]{1,0:T(8,128)(2,1)}, bf16[2048,256]{1,0:T(8,128)(2,1)S(1)}, u32[]{:S(2)}) copy-start(bf16[2048,256]{1,0:T(8,128)(2,1)S(1)} %fusion.5) | copy-start | bytes 3145732
  113.5 5.4 %copy-start.6 = (f32[11,256]{1,0:T(8,128)S(1)}, f32[11,256]{1,0:T(8,128)}, u32[]{:S(2)}) copy-start(f32[11,256]{1,0:T(8,128)} %param.18) | copy-start | bytes 33796
  118.9 3.6 %copy-start = (f32[2048,256]{1,0:T(8,128)S(1)}, f32[2048,256]{1,0:T(8,128)}, u32[]{:S(2)}) copy-start(f32[2048,256]{1,0:T(8,128)} %get-tuple-element.51) | copy-start | bytes 6291460
  122.4 7.8 %copy-start.9 = (f32[256]{0:T(256)S(1)}, f32[256]{0:T(256)}, u32[]{:S(2)}) copy-start(f32[256]{0:T(256)} %get-tuple-element.50) | copy-start | bytes 3076
  122.5 7.8 %copy-start.13 = (f32[256]{0:T(256)S(1)}, f32[256]{0:T(256)}, u32[]{:S(2)}) copy-start(f32[256]{0:T(256)} %fusion.6) | copy-start | bytes 3076
  122.5 7.8 %copy-start.18 = (f32[256]{0:T(256)S(1)}, f32[256]{0:T(256)}, u32[]{:S(2)}) copy-start(f32[256]{0:T(256)} %get-tuple-element.46) | copy-start | bytes 3076
  122.5 7.8 %copy-start.19 = (f32[256]{0:T(256)S(1)}, f32[256]{0:T(256)}, u32[]{:S(2)}) copy-start(f32[256]{0:T(256)} %get-tuple-element.48) | copy-start | bytes 3076
  122.5 7.8 %copy-start.10 = (f32[1,256]{1,0:T(1,128)S(1)}, f32[1,256]{1,0:T(1,128)}, u32[]{:S(2)}) copy-start(f32[1,256]{1,0:T(1,128)} %fusion.70) | copy-start | bytes 3076
  126.0 66.5 %all-to-all-start.3 = ((f32[16,1,256]{2,1,0:T(1,128)}), f32[16,1,256]{2,1,0:T(1,128)S(1)}, u32[]{:S(2)}, u32[]{:S(2)}) async-start(f32[16,1,256]{2,1,0:T(1,128)} %reshape.341), calls=%async_computation.3 | async-start | bytes 32768 | tf_op jit(solution)/shard_map/all_to_all | solution.py:121
  129.5 109.9 %all-reduce.4.cloned.1.call-start = ((), (), s32[]{:S(2)}) async-start(), calls=%async_computation.4 | async-start | bytes 1572864 | tf_op jit(solution)/shard_map/psum | solution.py:106
  198.5 5.3 %copy-start.15 = (s32[128]{0:T(128)S(1)}, s32[128]{0:T(128)}, u32[]{:S(2)}) copy-start(s32[128]{0:T(128)} %reshape.315) | copy-start | bytes 1540
  203.8 17.2 %copy-start.14 = (s32[128]{0:T(128)S(1)}, s32[128]{0:T(128)}, u32[]{:S(2)}) copy-start(s32[128]{0:T(128)} %reshape.307) | copy-start | bytes 1540
Sparse Core Ops, SparseCore 0:
  134.7 94.0 all-reduce.3
where the time goes:
time: 250 us; the launch traced here: 248 us
  blocking collectives  62.2 us (25%)
  other arithmetic  43 us (17%)
  waiting for transfers between devices  40.8 us (16%)
  matrix products  38.5 us (15%)
  starting transfers between devices  26.3 us (11%)
  local copies, waits for them, and re-layouts  22.8 us (9%)
  between operations  14.6 us (6%)
    psum x1, blocking collectives, shards(): lax.psum((input_term, bias_term, out_grad), 'wide')  62.2 us
    scatter-add x2, other arithmetic, shards(): jax.ops.segment_sum(contrib.reshape(slot_count, block_width, block_width)...  34.1 us
    all_to_all x1, waiting for transfers between devices, shards(): lax.all_to_all(send_ao, 'wide', split_axis=0, concat_axis=0, tiled=True)  33.2 us
    all_to_all x1, starting transfers between devices, shards(): lax.all_to_all(partial_value, 'wide', split_axis=0, concat_axis=0, tiled=...  11.2 us
    dot_general x2, matrix products, shards(): jnp.einsum('ncpm,ncpq->ncmq', weighted, recv_ao[:, :, entry_pos], preferr...  10.4 us
    all_to_all x1, starting transfers between devices, shards(): lax.all_to_all(send_ids, 'wide', split_axis=0, concat_axis=0, tiled=True)  7.36 us
    gather x2, local copies, waits for them, and re-layouts, owner_parts(): chosen = blocks[block_ids[:, :, entry_pos]]  6.06 us
    dot_general x3, matrix products, shards(): jnp.dot(grad_round, w_layers[layer_idx].T, preferred_element_type=jnp.flo...  5.1 us
  transfers between devices with their start and end apart: 5, of which 3 were waited for; matrix products, arithmetic and copies ran while one was open for 24% of the time, Pallas kernels for 0%

commit v1 on v0

v1 whole, which is shorter than its diff:
```python
import functools

import jax
import jax.numpy as jnp
from jax import lax
from jax.experimental import pallas as pl
from jax.experimental.pallas import tpu as pltpu
from jax.sharding import PartitionSpec as P

highest = lax.Precision.HIGHEST
F32 = jnp.float32
BF16 = jnp.bfloat16
CHUNK = 512
VMEM = pl.BlockSpec(memory_space=pltpu.VMEM)
SMEM = pl.BlockSpec(memory_space=pltpu.SMEM)
PARAMS = pltpu.CompilerParams(vmem_limit_bytes=56 * 1024 * 1024)


def up8(x):
    return (x + 7) // 8 * 8


def eye_mask(points):
    return lax.broadcasted_iota(jnp.int32, (points, 128), 0) == lax.broadcasted_iota(
        jnp.int32, (points, 128), 1
    )


def col_dot(a, b):
    return lax.dot_general(a, b, (((0,), (0,)), ((), ())), preferred_element_type=F32)


def rho_kernel(cap, pid_ref, ao_ref, den_ref, out_ref):
    sources = ao_ref.shape[0]
    points, width = ao_ref.shape[3:]
    me = lax.axis_index("wide")
    own = den_ref[:, pl.ds(pl.multiple_of(me * width, width), width)]
    eye = eye_mask(points)

    def body(i, carry):
        rows = []
        for r in range(cap):
            c = pid_ref[i, r]
            other = den_ref[:, pl.ds(pl.multiple_of(c * width, width), width)]
            x = ao_ref[i, r, 0]
            y = ao_ref[i, r, 1]
            q = jnp.dot(x, own, preferred_element_type=F32) * x.astype(F32)
            q = q + jnp.dot(x, other, preferred_element_type=F32) * y.astype(F32)
            col = jnp.sum(q, axis=1, keepdims=True)
            rows.append(jnp.sum(jnp.where(eye, col, 0.0), axis=0, keepdims=True))
        pad = out_ref.shape[1] - cap
        if pad:
            rows.append(jnp.zeros((pad, 128), F32))
        out_ref[i] = jnp.concatenate(rows, axis=0)
        return carry

    lax.fori_loop(0, sources, body, 0)


def mlp_kernel(
    slot_ref, src_ref, ret_ref, pre_ref, feat_ref, quad_ref, win_ref, bias_ref, wl_ref, wout_ref,
    sendw_ref, grads_ref, rho_scr, quad_scr, pw_scr,
):
    batches, points = quad_ref.shape
    hidden = wout_ref.shape[1]
    layers = wl_ref.shape[0]
    slots = ret_ref.shape[0]
    eye = eye_mask(points)
    slot_no = lax.broadcasted_iota(jnp.int32, (batches, slots), 1)
    pick = (slot_no == slot_ref[:, 0:1]) | (slot_no == slot_ref[:, 1:2])
    rho = jnp.dot(pick.astype(F32), ret_ref[...], precision=highest, preferred_element_type=F32)
    rho_scr[...] = rho
    quad_scr[...] = jnp.zeros_like(quad_scr)
    quad_scr[:, 0:points] = quad_ref[...]
    grads_ref[...] = jnp.zeros_like(grads_ref)
    per = CHUNK // points
    small = layers * hidden
    features = feat_ref.shape[0]
    feat_base = small
    bias_base = small + features
    out_row = bias_base + layers + 1

    def as_col(block):
        spread = jnp.where(eye[None], block[:, None, :], 0.0)
        return jnp.sum(spread, axis=2, keepdims=True).reshape(CHUNK, 1)

    def body(k, carry):
        at = pl.multiple_of(k * per, per)
        row = pl.multiple_of(k * CHUNK, CHUNK)
        rho_col = as_col(rho_scr[pl.ds(at, per), :])
        quad_col = as_col(quad_scr[pl.ds(at, per), :])
        pre = pre_ref[pl.ds(row, CHUNK), :] + rho_col * win_ref[0:1, :]
        acts = [jnp.tanh(pre).astype(BF16)]
        for l in range(layers):
            inner = jnp.dot(acts[-1], wl_ref[l], preferred_element_type=F32)
            acts.append(jnp.tanh(inner + bias_ref[l + 1 : l + 2, :]).astype(BF16))
        top = acts[-1].astype(F32)
        score = jnp.sum(top * wout_ref[...], axis=1, keepdims=True)
        enhance = 2.0 * jax.nn.sigmoid(score)
        grad_score = quad_col * rho_col * enhance * (1.0 - 0.5 * enhance)
        grads_ref[out_row : out_row + 1, :] += jnp.sum(grad_score * top, axis=0, keepdims=True)
        grad = grad_score * wout_ref[...]
        for l in reversed(range(layers)):
            after = acts[l + 1].astype(F32)
            grad = grad * (1.0 - after * after)
            rounded = grad.astype(BF16)
            grads_ref[l * hidden : (l + 1) * hidden, :] += col_dot(acts[l], rounded)
            b = bias_base + l + 1
            grads_ref[b : b + 1, :] += jnp.sum(grad, axis=0, keepdims=True)
            grad = lax.dot_general(
                rounded, wl_ref[l], (((1,), (1,)), ((), ())), preferred_element_type=F32
            )
        first = acts[0].astype(F32)
        grad = grad * (1.0 - first * first)
        grads_ref[bias_base : bias_base + 1, :] += jnp.sum(grad, axis=0, keepdims=True)
        grads_ref[feat_base : feat_base + 1, :] += jnp.sum(grad * rho_col, axis=0, keepdims=True)
        hi = grad.astype(BF16)
        lo = (grad - hi.astype(F32)).astype(BF16)
        feat = feat_ref[:, pl.ds(row, CHUNK)]
        fhi = feat.astype(BF16)
        flo = (feat - fhi.astype(F32)).astype(BF16)
        term = (
            jnp.dot(fhi, hi, preferred_element_type=F32)
            + jnp.dot(fhi, lo, preferred_element_type=F32)
            + jnp.dot(flo, hi, preferred_element_type=F32)
        )
        grads_ref[feat_base + 1 : feat_base + features, :] += term[1:features]
        grad_rho = jnp.sum(grad * win_ref[0:1, :], axis=1, keepdims=True)
        weight = (quad_col * enhance + grad_rho).reshape(per, points, 1)
        pw_scr[pl.ds(at, per), :] = jnp.sum(jnp.where(eye[None], weight, 0.0), axis=1)
        return carry

    lax.fori_loop(0, batches // per, body, 0)
    batch_no = lax.broadcasted_iota(jnp.int32, (slots, batches), 1)
    back = (batch_no == src_ref[...]).astype(F32)
    sendw_ref[...] = jnp.dot(back, pw_scr[...], precision=highest, preferred_element_type=F32)


def potential_kernel(cap, pid_ref, ao_ref, w_ref, out_ref, acc_ref):
    sources = ao_ref.shape[0]
    points, width = ao_ref.shape[3:]
    me = lax.axis_index("wide")
    eye = eye_mask(points)
    acc_ref[...] = jnp.zeros_like(acc_ref)

    def body(i, own):
        w = w_ref[i]
        xs, ws = [], []
        for r in range(cap):
            x = ao_ref[i, r, 0]
            col = jnp.sum(jnp.where(eye, w[r : r + 1, :], 0.0), axis=1, keepdims=True)
            xs.append(x)
            ws.append((x.astype(F32) * col).astype(BF16))
        for r in range(cap):
            c = pid_ref[i, r]
            acc_ref[c] += col_dot(ws[r], ao_ref[i, r, 1])
        return own + col_dot(jnp.concatenate(ws, axis=0), jnp.concatenate(xs, axis=0))

    own = lax.fori_loop(0, sources, body, jnp.zeros((width, width), F32))
    acc_ref[me] += own
    for c in range(acc_ref.shape[0]):
        out_ref[:, c * width : (c + 1) * width] = acc_ref[c].astype(out_ref.dtype)


def shards(
    density, ao_values, block_lists, counts, other_features, quad_weights, w_in, biases, w_layers,
    w_out,
):
    n = lax.axis_size("wide")
    batches, entries, points, width = ao_values.shape
    blocks = density.shape[1] // width
    cap = max(2, (batches * entries + blocks - 1) // blocks)
    capp = up8(cap)
    hidden = w_out.shape[0]
    layers = w_layers.shape[0]
    features = w_in.shape[0]
    total = batches * entries
    live = jnp.arange(entries)[None, :] < counts[:, None]
    masked = jnp.where(live[:, :, None, None], ao_values, jnp.zeros((), ao_values.dtype))
    masked = masked.reshape(total, points, width)
    target = block_lists.reshape(-1)
    ids = jnp.arange(total, dtype=jnp.int32)
    earlier = (target[:, None] == target[None, :]) & (ids[None, :] < ids[:, None])
    rank = jnp.sum(earlier.astype(jnp.int32), axis=1)
    slot_of = target * cap + rank
    table = slot_of[None, :] == jnp.arange(n * cap, dtype=jnp.int32)[:, None]
    filled = jnp.any(table, axis=1)
    source = jnp.sum(jnp.where(table, ids[None, :], 0), axis=1)
    partner = jnp.sum(
        jnp.where(table, jnp.flip(block_lists, 1).reshape(-1)[None, :], 0), axis=1
    )
    pairs = jnp.stack([source, source ^ 1], axis=1)
    send_ao = jnp.where(filled[:, None, None, None], masked[pairs], jnp.zeros((), masked.dtype))
    send_ao = send_ao.reshape(n, cap, 2, points, width)
    a2a = functools.partial(
        lax.all_to_all, axis_name="wide", split_axis=0, concat_axis=0, tiled=True
    )
    recv_ao = a2a(send_ao)
    recv_pid = a2a(partner.reshape(n, cap))
    parts = pl.pallas_call(
        functools.partial(rho_kernel, cap),
        out_shape=jax.ShapeDtypeStruct((n, capp, 128), F32),
        in_specs=[SMEM, VMEM, VMEM],
        out_specs=VMEM,
        compiler_params=PARAMS,
    )(recv_pid, recv_ao, density)
    returned = a2a(parts)
    rows = batches * points
    pre_other = (
        jnp.einsum("bfp,fh->bph", other_features, w_in[1:], precision=highest) + biases[0]
    ).reshape(rows, hidden)
    feat = jnp.concatenate(
        [
            jnp.zeros((1, rows), F32),
            other_features.transpose(1, 0, 2).reshape(features - 1, rows),
        ],
        axis=0,
    )
    slot_pad = (target * capp + rank).reshape(batches, entries)
    src_pad = jnp.where(filled, source // entries, -1).reshape(n, cap)
    src_pad = jnp.pad(src_pad, ((0, 0), (0, capp - cap)), constant_values=-1).reshape(n * capp, 1)
    grad_rows = up8(layers * hidden + features + layers + 2)
    send_w, grads = pl.pallas_call(
        mlp_kernel,
        out_shape=(
            jax.ShapeDtypeStruct((n * capp, 128), F32),
            jax.ShapeDtypeStruct((grad_rows, hidden), F32),
        ),
        in_specs=[VMEM] * 10,
        out_specs=(VMEM, VMEM),
        scratch_shapes=[pltpu.VMEM((batches, 128), F32)] * 3,
        compiler_params=PARAMS,
    )(
        slot_pad, src_pad, returned.reshape(n * capp, 128), pre_other, feat, quad_weights, w_in,
        biases, w_layers, w_out[None, :],
    )
    recv_w = a2a(send_w.reshape(n, capp, 128))
    grads = lax.psum(grads, "wide")
    potential = pl.pallas_call(
        functools.partial(potential_kernel, cap),
        out_shape=jax.ShapeDtypeStruct(density.shape, density.dtype),
        in_specs=[SMEM, VMEM, VMEM],
        out_specs=VMEM,
        scratch_shapes=[pltpu.VMEM((blocks, width, width), F32)],
        compiler_params=PARAMS,
    )(recv_pid, recv_ao, recv_w)
    base = layers * hidden
    return (
        potential,
        grads[:base].reshape(layers, hidden, hidden),
        grads[base : base + features],
        grads[base + features : base + features + layers + 1],
        grads[base + features + layers + 1],
    )


def solution(mesh):
    placed = (
        P(("groups", "wide"), None),
        P(("groups", "wide"), None, None, None),
        P(("groups", "wide"), None),
        P(("groups", "wide")),
        P(("groups", "wide"), None, None),
        P(("groups", "wide"), None),
        P(),
        P(),
        P(),
        P(),
    )
    return jax.shard_map(
        shards,
        mesh=mesh,
        in_specs=placed,
        out_specs=(
            P(("groups", "wide"), None),
            P("groups", None, None),
            P("groups", None),
            P("groups", None),
            P("groups"),
        ),
        check_vma=False,
    )
```

time: 250 us -> 211 us (0.84)
  waiting for transfers between devices: 40.8 us -> 111 us
  blocking collectives: 62.2 us -> 11.4 us
  other arithmetic: 43 us -> 5.44 us
  matrix products: 38.5 us -> 3.19 us
  Pallas kernels: 0 us -> 25.4 us
  local copies, waits for them, and re-layouts: 22.8 us -> 14.9 us
    psum x1, waiting for transfers between devices: 0.01 us -> 69.1 us  [shards(): grads = lax.psum(grads, 'wide')]
    psum x1 -> x0, blocking collectives: 62.2 us -> none  [shards(): lax.psum((input_term, bias_term, out_grad), 'wide')]
    dot_general x19 -> x1, matrix products: 38.5 us -> 3.19 us  [shards(): jnp.einsum('bfp,fh->bph', other_features, w_in[1:], precision=highest)]
    scatter-add x2 -> x0, other arithmetic: 34.1 us -> none  [shards(): jax.ops.segment_sum(contrib.reshape(slot_count, block_width, block_width)...]
    pallas_call x0 -> x3, Pallas kernels: none -> 25.4 us  [the longest x1 8.98 us: shards(): pl.pallas_call(mlp_kernel, out_shape=(jax.ShapeDtypeStruct((n * capp, 128...]
    all_to_all x0 -> x1, blocking collectives: none -> 11.4 us  [shards(): recv_w = a2a(send_w.reshape(n, capp, 128))]
    gather x8 -> x1, local copies, waits for them, and re-layouts: 9.67 us -> 1.01 us  [shards(): masked[pairs]]
    slice x2 -> x6, local copies, waits for them, and re-layouts: 0.6 us -> 5.94 us  [the longest x1 2.06 us: shards(): grads[:base].reshape(layers, hidden, hidden)]
  transfers between devices with their start and end apart: 5 -> 4, of which waited for: 3 -> 4; matrix products, arithmetic and copies ran while one was open for 24% -> 6% of each run, Pallas kernels for 0% -> 4%
where the time goes in v1:
time: 211 us; the launch traced here: 210 us
  waiting for transfers between devices  111 us (53%)
  Pallas kernels  25.4 us (12%)
  starting transfers between devices  24.5 us (12%)
  local copies, waits for them, and re-layouts  14.9 us (7%)
  between operations  14.2 us (7%)
  blocking collectives  11.4 us (5%)
  other arithmetic  5.44 us (3%)
  matrix products  3.19 us (2%)
    psum x1, waiting for transfers between devices, shards(): grads = lax.psum(grads, 'wide')  69.1 us
    all_to_all x1, waiting for transfers between devices, shards(): recv_ao = a2a(send_ao)  37.4 us
    all_to_all x1, blocking collectives, shards(): recv_w = a2a(send_w.reshape(n, capp, 128))  11.4 us
    all_to_all x1, starting transfers between devices, shards(): returned = a2a(parts)  11.2 us
    pallas_call x1, Pallas kernels, shards(): pl.pallas_call(mlp_kernel, out_shape=(jax.ShapeDtypeStruct((n * capp, 128...  8.98 us
    pallas_call x1, Pallas kernels, shards(): pl.pallas_call(functools.partial(potential_kernel, cap), out_shape=jax.Sh...  8.56 us
    pallas_call x1, Pallas kernels, shards(): pl.pallas_call(functools.partial(rho_kernel, cap), out_shape=jax.ShapeDty...  7.87 us
    all_to_all x1, starting transfers between devices, shards(): recv_pid = a2a(partner.reshape(n, cap))  7.36 us
  transfers between devices with their start and end apart: 4, of which 4 were waited for; matrix products, arithmetic and copies ran while one was open for 6% of the time, Pallas kernels for 4%

profile of v1, /device:TPU:0, one launch (start us, length us, event | category | flops | bytes accessed | tf_op | source)
XLA Modules:
  0.0 210.1 jit_solution(17168004081211452292)
XLA Ops:
  7.2 0.7 rev.4
  7.9 0.8 copy.84
  9.0 0.2 convert_reduce_fusion
  9.3 0.7 all_to_all.16
  10.0 7.4 %all-to-all-start = ((s32[16,1,8]{2,1,0:T(1,128)}), s32[16,1,8]{2,1,0:T(1,128)S(1)}, u32[]{:S(2)}, u32[]{:S(2)}) async-start(s32[16,1,8]{2,1,0:T(1,128)} %bitcast), calls=%async_computation | async-start | bytes 16384 | tf_op jit(solution)/shard_map/all_to_all | solution.py:199
  17.5 0.7 iota_compare_fusion.2
  18.6 0.7 fusion.1
  19.6 1.4 broadcast_select_fusion.1
  21.0 1.0 gather_fusion
  22.0 1.6 broadcast_select_fusion
  23.7 0.6 copy-done.3
  24.3 5.9 %all-to-all-start.1 = ((bf16[16,8,2,32,128]{4,3,2,1,0:T(8,128)(2,1)}), bf16[16,8,2,32,128]{4,3,2,1,0:T(8,128)(2,1)S(1)}, u32[]{:S(2)}, u32[]{:S(2)}) async-start(bf16[16,8,2,32,128]{4,3,2,1,0:T(8,128)(2,1)} %broadcast_select_fusion), calls=%async_computation.1 | async-start | bytes 4194304 | tf_op jit(solution)/shard_map/all_to_all | solution.py:198
  30.3 0.3 copy.97
  30.7 3.2 %convolution_add_fusion = f32[64,32,256]{2,1,0:T(8,128)} fusion(f32[64,10,32]{2,1,0:T(8,128)S(1)} %copy.97, f32[256]{0:T(256)S(1)} %bitcast.35, f32[11,256]{1,0:T(8,128)S(1)} %copy-done.4), kind=kOutput, calls=%fused_computation.2 | convolution fusion | flops 63438848 | bytes 2191360 | tf_op jit(solution)/shard_map/bfp,fh->bph/dot_general | solution.py:210
  33.9 37.4 %all-to-all-done.1.ao_ref = bf16[16,8,2,32,128]{4,3,2,1,0:T(8,128)(2,1)S(1)} async-done(((bf16[16,8,2,32,128]{4,3,2,1,0:T(8,128)(2,1)}), bf16[16,8,2,32,128]{4,3,2,1,0:T(8,128)(2,1)S(1)}, u32[]{:S(2)}, u32[]{:S(2)}) %all-to-all-start.1) | async-done | bytes 2097184 | tf_op jit(solution)/shard_map/all_to_all | solution.py:198
  71.3 1.3 copy-done
  72.6 7.9 %shard_map.137 = f32[16,8,128]{2,1,0:T(8,128)} custom-call(s32[16,8]{1,0:T(8,128)} %bitcast.32, bf16[16,8,2,32,128]{4,3,2,1,0:T(8,128)(2,1)} %copy-done, bf16[128,2048]{1,0:T(8,128)(2,1)} %den_ref.1), custom_call_target="tpu_custom_call" | custom-call | tf_op jit(solution)/shard_map/pallas_call | solution.py:200
  80.5 11.2 %all-to-all-start.2 = ((f32[16,8,128]{2,1,0:T(8,128)}), f32[16,8,128]{2,1,0:T(8,128)S(1)}, u32[]{:S(2)}, u32[]{:S(2)}) async-start(f32[16,8,128]{2,1,0:T(8,128)} %shard_map.137), calls=%async_computation.2 | async-start | bytes 131072 | tf_op jit(solution)/shard_map/all_to_all | solution.py:207
  91.9 0.7 copy.99.quad_ref
  92.7 0.2 reshape.223
  92.9 0.6 add.49.slot_ref
  93.5 0.7 concatenate.22.feat_ref
  94.2 4.4 %all-to-all-done.2 = f32[16,8,128]{2,1,0:T(8,128)S(1)} async-done(((f32[16,8,128]{2,1,0:T(8,128)}), f32[16,8,128]{2,1,0:T(8,128)S(1)}, u32[]{:S(2)}, u32[]{:S(2)}) %all-to-all-start.2) | async-done | bytes 65568 | tf_op jit(solution)/shard_map/all_to_all | solution.py:207
  98.6 0.6 copy-done.2
  99.3 9.0 %shard_map.138 = (f32[128,128]{1,0:T(8,128)}, f32[784,256]{1,0:T(8,128)}) custom-call(s32[64,2]{1,0:T(8,128)} %add.49.slot_ref, s32[128,1]{1,0:T(8,128)} %get-tuple-element.11.src_ref, f32[128,128]{1,0:T(8,128)} %bitcast.31, f32[2048,256]{1,0:T(8,128)} %bitcast.27, f32[11,2048]{1,0:T(8,128)} %concatenate.22.feat_ref, f32[64,32]{1,0:T(8,128)} %copy.99.quad_ref, ...), custom_call_target="tpu_custom_call" | custom-call | tf_op jit(solution)/shard_map/pallas_call | solution.py:223
  108.3 11.4 %all_to_all.26.w_ref = f32[16,8,128]{2,1,0:T(8,128)} all-to-all(f32[16,8,128]{2,1,0:T(8,128)} %bitcast.34), channel_id=1, replica_groups=mesh['groups'=2,'wide'=16] {'wide'}, dimensions={0} | all-to-all | bytes 131072 | tf_op jit(solution)/shard_map/all_to_all | solution.py:237
  119.7 8.6 %shard_map.139 = bf16[128,2048]{1,0:T(8,128)(2,1)} custom-call(s32[16,8]{1,0:T(8,128)} %bitcast.33, bf16[16,8,2,32,128]{4,3,2,1,0:T(8,128)(2,1)} %copy-done, f32[16,8,128]{2,1,0:T(8,128)} %all_to_all.26.w_ref), custom_call_target="tpu_custom_call" | custom-call | tf_op jit(solution)/shard_map/pallas_call | solution.py:239
  128.2 69.1 %all-reduce.3.cloned.1.call-done = f32[784,256]{1,0:T(8,128)} async-done(((f32[784,256]{1,0:T(8,128)}), f32[784,256]{1,0:T(8,128)}) %all-reduce.3.cloned.1.call-update) | async-done | bytes 802832 | tf_op jit(solution)/shard_map/psum | solution.py:238
  197.3 1.3 slice.29
  198.6 1.3 slice.28
  199.8 1.3 slice.27
  201.2 2.1 slice.26
  (33 shorter events, 1.8 us)
Async XLA Ops:
  10.0 13.7 %all-to-all-start = ((s32[16,1,8]{2,1,0:T(1,128)}), s32[16,1,8]{2,1,0:T(1,128)S(1)}, u32[]{:S(2)}, u32[]{:S(2)}) async-start(s32[16,1,8]{2,1,0:T(1,128)} %bitcast), calls=%async_computation | async-start | bytes 16384 | tf_op jit(solution)/shard_map/all_to_all | solution.py:199
  23.6 6.8 %copy-start.1 = (f32[64,10,32]{0,2,1:T(8,128)S(1)}, f32[64,10,32]{0,2,1:T(8,128)}, u32[]{:S(2)}) copy-start(f32[64,10,32]{0,2,1:T(8,128)} %param.14) | copy-start | bytes 245764
  23.6 7.1 %copy-start.4 = (f32[11,256]{1,0:T(8,128)S(1)}, f32[11,256]{1,0:T(8,128)}, u32[]{:S(2)}) copy-start(f32[11,256]{1,0:T(8,128)} %win_ref.1) | copy-start | bytes 33796
  23.6 7.1 %slice-start = ((f32[4,256]{1,0:T(4,128)}), f32[1,256]{1,0:T(1,128)S(1)}, s32[]{:S(2)}) async-start(f32[4,256]{1,0:T(4,128)} %bias_ref.1), calls=%async_computation.5 | async-start | bytes 2048 | tf_op jit(solution)/shard_map/slice | solution.py:210
  23.7 0.6 copy-start.3
  24.3 47.0 %all-to-all-start.1 = ((bf16[16,8,2,32,128]{4,3,2,1,0:T(8,128)(2,1)}), bf16[16,8,2,32,128]{4,3,2,1,0:T(8,128)(2,1)S(1)}, u32[]{:S(2)}, u32[]{:S(2)}) async-start(bf16[16,8,2,32,128]{4,3,2,1,0:T(8,128)(2,1)} %broadcast_select_fusion), calls=%async_computation.1 | async-start | bytes 4194304 | tf_op jit(solution)/shard_map/all_to_all | solution.py:198
  30.6 61.1 %copy-start.6 = (s32[64,2]{0,1:T(2,128)S(1)}, s32[64,2]{0,1:T(2,128)}, u32[]{:S(2)}) copy-start(s32[64,2]{0,1:T(2,128)} %param.12) | copy-start | bytes 1540
  30.7 61.2 %copy-start.5 = (f32[64,32]{0,1:T(8,128)S(1)}, f32[64,32]{0,1:T(8,128)}, u32[]{:S(2)}) copy-start(f32[64,32]{0,1:T(8,128)} %param.15) | copy-start | bytes 24580
  71.3 1.3 copy-start
  80.5 18.1 %all-to-all-start.2 = ((f32[16,8,128]{2,1,0:T(8,128)}), f32[16,8,128]{2,1,0:T(8,128)S(1)}, u32[]{:S(2)}, u32[]{:S(2)}) async-start(f32[16,8,128]{2,1,0:T(8,128)} %shard_map.137), calls=%async_computation.2 | async-start | bytes 131072 | tf_op jit(solution)/shard_map/all_to_all | solution.py:207
  91.7 105.6 %all-reduce.3.cloned.1.call-start = ((), (), s32[]{:S(2)}) async-start(), calls=%async_computation.4 | async-start | bytes 1605632 | tf_op jit(solution)/shard_map/psum | solution.py:238
  98.6 0.6 copy-start.2
Sparse Core Ops, SparseCore 0:
  108.4 88.8 all-reduce.2

commit v2 on v1

v2 whole, which is shorter than its diff:
```python
import functools

import jax
import jax.numpy as jnp
from jax import lax
from jax.experimental import pallas as pl
from jax.experimental.pallas import tpu as pltpu
from jax.sharding import PartitionSpec as P

highest = lax.Precision.HIGHEST
F32 = jnp.float32
BF16 = jnp.bfloat16
CHUNK = 512
VMEM = pl.BlockSpec(memory_space=pltpu.VMEM)
SMEM = pl.BlockSpec(memory_space=pltpu.SMEM)


def up8(x):
    return (x + 7) // 8 * 8


def eye_mask(points):
    return lax.broadcasted_iota(jnp.int32, (points, 128), 0) == lax.broadcasted_iota(
        jnp.int32, (points, 128), 1
    )


def col_dot(a, b):
    return lax.dot_general(a, b, (((0,), (0,)), ((), ())), preferred_element_type=F32)


def fused_kernel(
    cap, chunk_rows,
    src_ref, mate_ref, lo_ref, lp_ref, pidmsg_ref, ao_ref, den_ref, slot_ref, srcpad_ref, feat_ref, quad_ref,
    win_ref, bias_ref, wl_ref, wout_ref,
    pot_ref, gw_ref, gin_ref, gbias_ref, gout_ref,
    send_ao, recv_ao, recv_pid, table, stable, send_part, ret, pre_scr, rho_scr, quad_scr, pw_scr,
    small, grads, send_w, recv_w, send_g, recv_g, send_a, recv_a, send_s, recv_s, prefix, den,
    ssem, rsem, tsem,
):
    n = send_part.shape[0]
    points, width = ao_ref.shape[1:]
    batches = quad_ref.shape[0]
    hidden = wout_ref.shape[1]
    layers = wl_ref.shape[0]
    features = feat_ref.shape[0]
    halves = hidden // 128
    slots = n * cap
    capp = send_part.shape[1]
    blocks = den_ref.shape[1] // width
    me = lax.axis_index("wide")
    eye = eye_mask(points)

    def peer(d):
        return lax.rem(me + d, n)

    def origin(d):
        return lax.rem(me + n - d, n)

    def mine(k):
        return pl.ds(k * cap, cap)

    def copy(phase, src, dst, d):
        return pltpu.make_async_remote_copy(
            src_ref=src, dst_ref=dst, send_sem=ssem.at[phase, d], recv_sem=rsem.at[phase, d],
            device_id={"wide": peer(d)}, device_id_type=pl.DeviceIdType.MESH,
        )

    def each(fn):
        def body(d, carry):
            fn(d)
            return carry

        lax.fori_loop(1, n, body, 0)

    barrier = pltpu.get_barrier_semaphore()

    def greet(d):
        pl.semaphore_signal(
            barrier, inc=1, device_id={"wide": peer(d)}, device_id_type=pl.DeviceIdType.MESH
        )

    each(greet)

    def fill(k):
        for r in range(cap):
            e = src_ref[k, r]
            own = ao_ref[e].astype(F32) * lo_ref[k, r].astype(F32)
            mate = mate_ref[k, r]
            other = ao_ref[mate].astype(F32) * lp_ref[k, r].astype(F32)
            send_ao[k * cap + r, 0] = own.astype(BF16)
            send_ao[k * cap + r, 1] = other.astype(BF16)

    def pid_copy(d):
        return copy(0, pidmsg_ref.at[peer(d)], recv_pid.at[me], d)

    def pid_back(d):
        return copy(0, pidmsg_ref.at[peer(d)], recv_pid.at[origin(d)], d)

    def ao_copy(d):
        return copy(1, send_ao.at[mine(peer(d))], recv_ao.at[mine(me)], d)

    def ao_back(d):
        return copy(1, send_ao.at[mine(peer(d))], recv_ao.at[mine(origin(d))], d)

    pl.semaphore_wait(barrier, n - 1)
    each(lambda d: pid_copy(d).start())

    def send_one(d):
        fill(peer(d))
        ao_copy(d).start()

    each(send_one)
    fill(me)
    recv_ao[mine(me)] = send_ao[mine(me)]
    recv_pid[me] = pidmsg_ref[me]

    def den_body(c, carry):
        den[c] = den_ref[:, pl.ds(pl.multiple_of(c * width, width), width)]
        return carry

    lax.fori_loop(0, blocks, den_body, 0)
    per = CHUNK // points
    quad_scr[...] = jnp.zeros_like(quad_scr)
    quad_scr[:, 0:points] = quad_ref[...]
    grads[...] = jnp.zeros_like(grads)
    small[...] = jnp.zeros_like(small)

    def pre_body(k, carry):
        row = pl.multiple_of(k * CHUNK, CHUNK)
        part = lax.dot_general(
            feat_ref[:, pl.ds(row, CHUNK)], win_ref[...], (((0,), (0,)), ((), ())),
            precision=highest, preferred_element_type=F32,
        )
        pre_scr[pl.ds(row, CHUNK), :] = part + bias_ref[0:1, :]
        return carry

    lax.fori_loop(0, batches // per, pre_body, 0)

    each(lambda d: pid_back(d).wait_recv())
    pid_row = lax.fori_loop(
        0, n, lambda i, a: a + recv_pid[i], jnp.zeros(recv_pid.shape[1:], jnp.int32)
    )[0:1, :]
    up = lax.broadcasted_iota(jnp.int32, (slots, slots), 0)
    across = lax.broadcasted_iota(jnp.int32, (slots, slots), 1)
    pid_col = jnp.sum(jnp.where(up == across, pid_row, 0), axis=1, keepdims=True)
    twin = (pid_row == pid_col) & (across < up)
    order = jnp.sum(((pid_row < pid_col) | twin).astype(jnp.int32), axis=1, keepdims=True)
    held = jnp.max(twin.astype(jnp.int32), axis=1, keepdims=True)
    placed = order == across
    table[...] = jnp.zeros_like(table)
    table[0:1, :] = pid_row
    table[1:2, :] = jnp.sum(jnp.where(placed, up, 0), axis=0, keepdims=True)
    table[2:3, :] = jnp.sum(jnp.where(placed, held, 0), axis=0, keepdims=True)
    upto = jnp.sum((pid_col <= across).astype(jnp.int32), axis=0, keepdims=True)
    table[3:4, :] = jnp.maximum(upto - 1, 0)
    table[4:5, :] = jnp.max((pid_col == across).astype(jnp.int32), axis=0, keepdims=True)
    to_scalar = pltpu.make_async_copy(table, stable, tsem.at[0])
    to_scalar.start()
    to_scalar.wait()

    own = den[me]

    def shares(i):
        rows = []
        for r in range(cap):
            c = stable[0, i * cap + r]
            other = den[c]
            x = recv_ao[i * cap + r, 0]
            y = recv_ao[i * cap + r, 1]
            q = jnp.dot(x, own, preferred_element_type=F32) * x.astype(F32)
            q = q + jnp.dot(x, other, preferred_element_type=F32) * y.astype(F32)
            col = jnp.sum(q, axis=1, keepdims=True)
            rows.append(jnp.sum(jnp.where(eye, col, 0.0), axis=0, keepdims=True))
        if capp > cap:
            rows.append(jnp.zeros((capp - cap, 128), F32))
        return jnp.concatenate(rows, axis=0)

    def part_copy(d):
        return copy(2, send_part.at[peer(d)], ret.at[me], d)

    def part_back(d):
        return copy(2, send_part.at[peer(d)], ret.at[origin(d)], d)

    ret[me] = shares(me)

    def answer(d):
        src = origin(d)
        ao_back(d).wait_recv()
        send_part[src] = shares(src)
        copy(2, send_part.at[src], ret.at[me], n - d).start()

    each(answer)
    each(lambda d: part_back(d).wait_recv())

    slot_no = lax.broadcasted_iota(jnp.int32, (batches, n * capp), 1)
    pick = (slot_no == slot_ref[:, 0:1]) | (slot_no == slot_ref[:, 1:2])
    rho_scr[...] = jnp.dot(
        pick.astype(F32), ret[...].reshape(n * capp, 128), precision=highest,
        preferred_element_type=F32,
    )
    bias_base = features
    out_row = bias_base + layers + 1

    def as_col(block):
        spread = jnp.where(eye[None], block[:, None, :], 0.0)
        return jnp.sum(spread, axis=2, keepdims=True).reshape(CHUNK, 1)

    def body(k, carry):
        at = pl.multiple_of(k * per, per)
        row = pl.multiple_of(k * CHUNK, CHUNK)
        rho_col = as_col(rho_scr[pl.ds(at, per), :])
        quad_col = as_col(quad_scr[pl.ds(at, per), :])
        pre = pre_scr[pl.ds(row, CHUNK), :] + rho_col * win_ref[0:1, :]
        acts = [jnp.tanh(pre).astype(BF16)]
        for l in range(layers):
            inner = jnp.dot(acts[-1], wl_ref[l], preferred_element_type=F32)
            acts.append(jnp.tanh(inner + bias_ref[l + 1 : l + 2, :]).astype(BF16))
        top = acts[-1].astype(F32)
        score = jnp.sum(top * wout_ref[...], axis=1, keepdims=True)
        enhance = 2.0 * jax.nn.sigmoid(score)
        grad_score = quad_col * rho_col * enhance * (1.0 - 0.5 * enhance)
        small[out_row : out_row + 1, :] += jnp.sum(grad_score * top, axis=0, keepdims=True)
        grad = grad_score * wout_ref[...]
        for l in reversed(range(layers)):
            after = acts[l + 1].astype(F32)
            grad = grad * (1.0 - after * after)
            rounded = grad.astype(BF16)
            grads[l * hidden : (l + 1) * hidden, :] += col_dot(acts[l], rounded)
            b = bias_base + l + 1
            small[b : b + 1, :] += jnp.sum(grad, axis=0, keepdims=True)
            grad = lax.dot_general(
                rounded, wl_ref[l], (((1,), (1,)), ((), ())), preferred_element_type=F32
            )
        first = acts[0].astype(F32)
        grad = grad * (1.0 - first * first)
        small[bias_base : bias_base + 1, :] += jnp.sum(grad, axis=0, keepdims=True)
        small[0:1, :] += jnp.sum(grad * rho_col, axis=0, keepdims=True)
        hi = grad.astype(BF16)
        lo = (grad - hi.astype(F32)).astype(BF16)
        feat = feat_ref[:, pl.ds(row, CHUNK)]
        fhi = feat.astype(BF16)
        flo = (feat - fhi.astype(F32)).astype(BF16)
        term = (
            jnp.dot(fhi, hi, preferred_element_type=F32)
            + jnp.dot(fhi, lo, preferred_element_type=F32)
            + jnp.dot(flo, hi, preferred_element_type=F32)
        )
        small[1:features, :] += term[1:features]
        grad_rho = jnp.sum(grad * win_ref[0:1, :], axis=1, keepdims=True)
        weight = (quad_col * enhance + grad_rho).reshape(per, points, 1)
        pw_scr[pl.ds(at, per), :] = jnp.sum(jnp.where(eye[None], weight, 0.0), axis=1)
        return carry

    lax.fori_loop(0, batches // per, body, 0)
    batch_no = lax.broadcasted_iota(jnp.int32, (n * capp, batches), 1)
    back = (batch_no == srcpad_ref[...]).astype(F32)
    send_w[:, capp:, :] = jnp.zeros((n, 8, 128), F32)
    send_w[:, 0:capp, :] = jnp.dot(
        back, pw_scr[...], precision=highest, preferred_element_type=F32
    ).reshape(n, capp, 128)
    small_rows = out_row + 1
    for k in range(small_rows):
        for h in range(halves):
            send_w[k, capp + h : capp + h + 1, :] = small[k : k + 1, h * 128 : (h + 1) * 128]

    def w_copy(d):
        return copy(3, send_w.at[peer(d)], recv_w.at[me], d)

    def w_back(d):
        return copy(3, send_w.at[peer(d)], recv_w.at[origin(d)], d)

    def g_copy(d):
        return copy(4, send_g.at[peer(d)], recv_g.at[me], d)

    def g_back(d):
        return copy(4, send_g.at[peer(d)], recv_g.at[origin(d)], d)

    def a_copy(d):
        return copy(5, send_a, recv_a.at[me], d)

    def a_back(d):
        return copy(5, send_a, recv_a.at[origin(d)], d)

    def s_copy(d):
        return copy(6, send_s, recv_s.at[me], d)

    def s_back(d):
        return copy(6, send_s, recv_s.at[origin(d)], d)

    each(lambda d: w_copy(d).start())

    def send_grad(d):
        k = peer(d)
        at = pl.multiple_of(k * chunk_rows, 16)
        send_g[k] = grads[pl.ds(at, chunk_rows), :].astype(BF16)
        g_copy(d).start()

    each(send_grad)
    recv_w[me] = send_w[me]
    each(lambda d: w_back(d).wait_recv())
    send_s[...] = lax.fori_loop(
        0, n, lambda i, a: a + recv_w[i, capp:, :], jnp.zeros((8, 128), F32)
    )
    each(lambda d: s_copy(d).start())

    def own_body(i, acc):
        w = recv_w[i]
        xs, ws = [], []
        for r in range(cap):
            x = recv_ao[i * cap + r, 0]
            col = jnp.sum(jnp.where(eye, w[r : r + 1, :], 0.0), axis=1, keepdims=True)
            weighted = (x.astype(F32) * col).astype(BF16)
            send_ao[i * cap + r, 0] = weighted
            xs.append(x)
            ws.append(weighted)
        return acc + col_dot(jnp.concatenate(ws, axis=0), jnp.concatenate(xs, axis=0))

    each(lambda d: ao_copy(d).wait_send())
    own_sum = lax.fori_loop(0, n, own_body, jnp.zeros((width, width), F32))
    group = 8

    def sorted_body(g, acc):
        for u in range(group):
            j = g * group + u
            s = stable[1, j]
            part = col_dot(send_ao[s, 0], recv_ao[s, 1])
            acc = acc * stable[2, j].astype(F32) + part
            prefix[j] = acc
        return acc

    lax.fori_loop(0, slots // group, sorted_body, jnp.zeros((width, width), F32))

    at = pl.multiple_of(me * chunk_rows, 16)
    each(lambda d: g_back(d).wait_recv())
    total = grads[pl.ds(at, chunk_rows), :]
    recv_g[me] = jnp.zeros(recv_g.shape[1:], BF16)
    total = lax.fori_loop(0, n, lambda i, a: a + recv_g[i].astype(F32), total)
    send_a[...] = total.astype(BF16)
    each(lambda d: a_copy(d).start())

    def out_body(c, carry):
        end = stable[3, c]
        value = prefix[end] * stable[4, c].astype(F32)
        value = value + own_sum * (c == me).astype(F32)
        pot_ref[:, pl.ds(pl.multiple_of(c * width, width), width)] = value.astype(pot_ref.dtype)
        return carry

    lax.fori_loop(0, blocks, out_body, 0)
    recv_a[me] = send_a[...]
    recv_s[me] = send_s[...]
    each(lambda d: s_back(d).wait_recv())
    for k in range(small_rows):
        row = jnp.concatenate([recv_s[k, h : h + 1, :] for h in range(halves)], axis=1)
        if k < features:
            gin_ref[k : k + 1, :] = row
        elif k < out_row:
            gbias_ref[k - features : k - features + 1, :] = row
        else:
            gout_ref[...] = row
    each(lambda d: a_back(d).wait_recv())

    def gw_body(k, carry):
        at = pl.multiple_of(k * chunk_rows, 16)
        gw_ref[pl.ds(at, chunk_rows), :] = recv_a[k].astype(F32)
        return carry

    lax.fori_loop(0, layers * hidden // chunk_rows, gw_body, 0)

    def drain(d):
        pid_copy(d).wait_send()
        part_copy(d).wait_send()
        w_copy(d).wait_send()
        g_copy(d).wait_send()
        a_copy(d).wait_send()
        s_copy(d).wait_send()

    each(drain)


def shards(
    density, ao_values, block_lists, counts, other_features, quad_weights, w_in, biases, w_layers,
    w_out,
):
    n = lax.axis_size("wide")
    me = lax.axis_index("wide")
    batches, entries, points, width = ao_values.shape
    blocks = density.shape[1] // width
    cap = max(2, (batches * entries + blocks - 1) // blocks)
    capp = up8(cap)
    slots = n * cap
    hidden = w_out.shape[0]
    layers = w_layers.shape[0]
    features = w_in.shape[0]
    total = batches * entries
    rows = batches * points
    target = block_lists.reshape(-1)
    ids = jnp.arange(total, dtype=jnp.int32)
    earlier = (target[:, None] == target[None, :]) & (ids[None, :] < ids[:, None])
    rank = jnp.sum(earlier.astype(jnp.int32), axis=1)
    slot_of = target * cap + rank
    table = slot_of[None, :] == jnp.arange(slots, dtype=jnp.int32)[:, None]
    live = (jnp.arange(entries)[None, :] < counts[:, None]).astype(jnp.int32)

    def at_slot(values):
        return jnp.sum(jnp.where(table, values.reshape(-1)[None, :], 0), axis=1).reshape(n, cap)

    source = at_slot(ids)
    partner = at_slot(jnp.flip(block_lists, 1))
    live_own = at_slot(live)
    live_other = at_slot(jnp.flip(live, 1))
    filled = jnp.any(table, axis=1).reshape(n, cap)
    lane = jnp.arange(slots, dtype=jnp.int32)
    spread = jnp.where(lane[None, :] // cap == me, jnp.tile(partner, (1, n)), 0)
    pid_msg = jnp.broadcast_to(spread[:, None, :], (n, 8, slots))
    feat = jnp.concatenate(
        [
            jnp.zeros((1, rows), F32),
            other_features.transpose(1, 0, 2).reshape(features - 1, rows),
        ],
        axis=0,
    )
    slot_pad = (target * capp + rank).reshape(batches, entries)
    src_pad = jnp.where(filled, source // entries, -1)
    src_pad = jnp.pad(src_pad, ((0, 0), (0, capp - cap)), constant_values=-1).reshape(n * capp, 1)
    weight_rows = layers * hidden
    chunk_rows = (-(-weight_rows // n) + 15) // 16 * 16
    while weight_rows % chunk_rows:
        chunk_rows += 16
    small_rows = up8(features + layers + 2)
    vm = pltpu.VMEM
    potential, gw, gin, gbias, gout = pl.pallas_call(
        functools.partial(fused_kernel, cap, chunk_rows),
        out_shape=(
            jax.ShapeDtypeStruct(density.shape, density.dtype),
            jax.ShapeDtypeStruct((weight_rows, hidden), F32),
            jax.ShapeDtypeStruct((features, hidden), F32),
            jax.ShapeDtypeStruct((layers + 1, hidden), F32),
            jax.ShapeDtypeStruct((1, hidden), F32),
        ),
        in_specs=[SMEM] * 4 + [VMEM] * 11,
        out_specs=(VMEM,) * 5,
        scratch_shapes=[
            vm((slots, 2, points, width), BF16),
            vm((slots, 2, points, width), BF16),
            vm((n, 8, slots), jnp.int32),
            vm((8, slots), jnp.int32),
            pltpu.SMEM((8, slots), jnp.int32),
            vm((n, capp, 128), F32),
            vm((n, capp, 128), F32),
            vm((rows, hidden), F32),
            vm((batches, 128), F32),
            vm((batches, 128), F32),
            vm((batches, 128), F32),
            vm((small_rows, hidden), F32),
            vm((n * chunk_rows, hidden), F32),
            vm((n, capp + 8, 128), F32),
            vm((n, capp + 8, 128), F32),
            vm((n, chunk_rows, hidden), BF16),
            vm((n, chunk_rows, hidden), BF16),
            vm((chunk_rows, hidden), BF16),
            vm((n, chunk_rows, hidden), BF16),
            vm((8, 128), F32),
            vm((n, 8, 128), F32),
            vm((slots, width, width), F32),
            vm((blocks, width, width), BF16),
            pltpu.SemaphoreType.DMA((7, n)),
            pltpu.SemaphoreType.DMA((7, n)),
            pltpu.SemaphoreType.DMA((1,)),
        ],
        compiler_params=pltpu.CompilerParams(
            vmem_limit_bytes=56 * 1024 * 1024, collective_id=0, has_side_effects=True
        ),
    )(
        source, source ^ 1, live_own, live_other, pid_msg, ao_values.reshape(total, points, width), density,
        slot_pad, src_pad, feat, quad_weights, w_in, biases, w_layers, w_out[None, :],
    )
    return (potential, gw.reshape(layers, hidden, hidden), gin, gbias, gout.reshape(hidden))


def solution(mesh):
    placed = (
        P(("groups", "wide"), None),
        P(("groups", "wide"), None, None, None),
        P(("groups", "wide"), None),
        P(("groups", "wide")),
        P(("groups", "wide"), None, None),
        P(("groups", "wide"), None),
        P(),
        P(),
        P(),
        P(),
    )
    return jax.shard_map(
        shards,
        mesh=mesh,
        in_specs=placed,
        out_specs=(
            P(("groups", "wide"), None),
            P("groups", None, None),
            P("groups", None),
            P("groups", None),
            P("groups"),
        ),
        check_vma=False,
    )
```

time: 211 us -> 111 us (0.53)
  waiting for transfers between devices: 111 us -> 0 us
  Pallas kernels: 25.4 us -> 93.8 us
  starting transfers between devices: 24.5 us -> 0 us
  between operations: 14.2 us -> 0.76 us
  blocking collectives: 11.4 us -> 0 us
  matrix products: 3.19 us -> 0 us
  local copies, waits for them, and re-layouts: 14.9 us -> 11.9 us
  other arithmetic: 5.44 us -> 2.48 us
    psum x1 -> x0, waiting for transfers between devices: 69.1 us -> none  [shards(): grads = lax.psum(grads, 'wide')]
    pallas_call x3 -> x1, Pallas kernels: 25.4 us -> 93.8 us  [shards(): pl.pallas_call(functools.partial(fused_kernel, cap, chunk_rows), out_shap...]
    all_to_all x3 -> x0, waiting for transfers between devices: 42 us -> none  [the longest x1 37.4 us: shards(): recv_ao = a2a(send_ao)]
    all_to_all x3 -> x0, starting transfers between devices: 24.4 us -> none  [the longest x1 11.2 us: shards(): returned = a2a(parts)]
    all_to_all x1 -> x0, blocking collectives: 11.4 us -> none  [shards(): recv_w = a2a(send_w.reshape(n, capp, 128))]
    slice x6 -> x0, local copies, waits for them, and re-layouts: 5.94 us -> none  [the longest x1 2.06 us: shards(): grads[:base].reshape(layers, hidden, hidden)]
    dot_general x1 -> x0, matrix products: 3.19 us -> none  [shards(): jnp.einsum('bfp,fh->bph', other_features, w_in[1:], precision=highest)]
    unnamed x17 -> x25, local copies, waits for them, and re-layouts: 4.33 us -> 7.35 us
  transfers between devices with their start and end apart: 4 -> 0, of which waited for: 4 -> 0; matrix products, arithmetic and copies ran while one was open for 6% -> 0% of each run, Pallas kernels for 4% -> 0%
where the time goes in v2:
time: 111 us; the launch traced here: 109 us
  Pallas kernels  93.8 us (85%)
  local copies, waits for them, and re-layouts  11.9 us (11%)
  other arithmetic  2.48 us (2%)
    pallas_call x1, Pallas kernels, shards(): pl.pallas_call(functools.partial(fused_kernel, cap, chunk_rows), out_shap...  93.8 us
    unnamed x25, local copies, waits for them, and re-layouts  7.35 us

profile of v2, /device:TPU:0, one launch (start us, length us, event | category | flops | bytes accessed | tf_op | source)
XLA Modules:
  0.0 108.9 jit_solution(7022589003202434631)
XLA Ops:
  0.7 0.7 copy-done.5
  1.4 0.1 copy.53
  1.5 0.1 broadcast_in_dim.69
  1.6 0.1 copy.56
  1.7 0.6 copy-done.8
  2.3 0.1 reshape.193
  2.6 0.1 broadcast_in_dim.66
  2.7 0.6 copy-done.3
  3.3 0.7 copy.63.quad_ref
  4.0 0.1 copy.52
  4.1 0.1 reshape.185
  4.2 0.2 convert_reduce_fusion
  4.4 0.1 fusion.2
  4.5 0.2 select_reduce_fusion
  4.9 0.6 broadcast_xor_fusion.mate_ref
  5.5 0.7 reshape.188.lp_ref
  6.2 0.7 reshape.187.lo_ref
  6.9 0.1 copy.61
  7.0 0.1 reduce_sum.54
  7.2 0.6 add.28.slot_ref
  7.9 0.7 broadcast_in_dim.72.pidmsg_ref
  8.6 0.1 copy.57
  8.7 0.7 fusion.1.srcpad_ref
  9.4 0.2 copy.62
  9.5 0.2 reshape.190
  9.7 0.7 concatenate.3.feat_ref
  10.4 93.8 %shard_map.137 = (bf16[128,2048]{1,0:T(8,128)(2,1)}, f32[768,256]{1,0:T(8,128)}, f32[11,256]{1,0:T(8,128)}, f32[4,256]{1,0:T(4,128)}, f32[1,256]{1,0:T(1,128)}) custom-call(s32[16,8]{1,0:T(8,128)} %copy-done.2, s32[16,8]{1,0:T(8,128)} %broadcast_xor_fusion.mate_ref, s32[16,8]{1,0:T(8,128)} %reshape.187.lo_ref, s32[16,8]{1,0:T(8,128)} %reshape.188.lp_ref, ...), custom_call_target="tpu_custom_call" | custom-call | tf_op jit(solution)/shard_map/pallas_call | solution.py:432
  104.2 2.0 %copy.69 = bf16[128,2048]{1,0:T(8,128)(2,1)} copy(bf16[128,2048]{1,0:T(8,128)(2,1)} %get-tuple-element.24) | data formatting | bytes 1048576
  106.1 0.9 copy.70
  107.0 0.6 copy.71
  107.7 0.6 copy.72
  108.4 0.6 copy.73
  (26 shorter events, 0.7 us)
Async XLA Ops:
  0.6 0.7 copy-start.5
  1.6 0.7 copy-start.8
  2.5 0.7 copy-start.3
  4.9 0.6 copy-start.2
  7.9 1.5 %copy-start.1 = (f32[64,10,32]{0,2,1:T(8,128)S(1)}, f32[64,10,32]{0,2,1:T(8,128)}, u32[]{:S(2)}) copy-start(f32[64,10,32]{0,2,1:T(8,128)} %param.14) | copy-start | bytes 245764
  104.2 2.0 %copy-start = (f32[768,256]{1,0:T(8,128)S(1)}, f32[768,256]{1,0:T(8,128)}, u32[]{:S(2)}) copy-start(f32[768,256]{1,0:T(8,128)} %get-tuple-element.11) | copy-start | bytes 2359300
  106.1 0.9 copy-start.4
  107.0 0.7 copy-start.6
  107.7 0.7 copy-start.7

commit v3 on v2

--- a/solution.py
+++ b/solution.py
@@ -31,10 +31,10 @@
 
 def fused_kernel(
     cap, chunk_rows,
-    src_ref, mate_ref, lo_ref, lp_ref, pidmsg_ref, ao_ref, den_ref, slot_ref, srcpad_ref, feat_ref, quad_ref,
+    list_ref, count_ref, ao_ref, den_ref, feat_ref, quad_ref,
     win_ref, bias_ref, wl_ref, wout_ref,
     pot_ref, gw_ref, gin_ref, gbias_ref, gout_ref,
-    send_ao, recv_ao, recv_pid, table, stable, send_part, ret, pre_scr, rho_scr, quad_scr, pw_scr,
+    send_ao, recv_ao, pid_msg, recv_pid, table, plan, splan, pick_scr, stable, send_part, ret, pre_scr, rho_scr, quad_scr, pw_scr,
     small, grads, send_w, recv_w, send_g, recv_g, send_a, recv_a, send_s, recv_s, prefix, den,
     ssem, rsem, tsem,
 ):
@@ -81,21 +81,59 @@
         )
 
     each(greet)
+    total = batches * 2
+    up = lax.broadcasted_iota(jnp.int32, (total, total), 0)
+    across = lax.broadcasted_iota(jnp.int32, (total, total), 1)
+    first_ids = list_ref[:, 0:1]
+    second_ids = list_ref[:, 1:2]
+    target = jnp.concatenate([first_ids, second_ids], axis=0)
+    partner = jnp.concatenate([second_ids, first_ids], axis=0)
+    target_row = jnp.sum(jnp.where(up == across, target, 0), axis=0, keepdims=True)
+    earlier = (target_row == target) & (across < up)
+    rank = jnp.sum(earlier.astype(jnp.int32), axis=1, keepdims=True)
+    square = (batches, batches)
+    same = lax.broadcasted_iota(jnp.int32, square, 0) == lax.broadcasted_iota(jnp.int32, square, 1)
+    used = jnp.sum(jnp.where(same, count_ref[...], 0), axis=1, keepdims=True)
+    used = jnp.concatenate([used, used], axis=0)
+    entry = lax.broadcasted_iota(jnp.int32, (total, 1), 0)
+    second = (entry >= batches).astype(jnp.int32)
+    source = 2 * (entry - batches * second) + second
+    mate_entry = source + 1 - 2 * second
+    slot_no = lax.broadcasted_iota(jnp.int32, (total, slots), 1)
+    sits = slot_no == target * cap + rank
+
+    def at_slot(values):
+        return jnp.sum(jnp.where(sits, values, 0), axis=0, keepdims=True)
+
+    plan[...] = jnp.zeros_like(plan)
+    plan[0:1, :] = at_slot(source)
+    plan[1:2, :] = at_slot(mate_entry)
+    plan[2:3, :] = at_slot((second < used).astype(jnp.int32))
+    plan[3:4, :] = at_slot((1 - second < used).astype(jnp.int32))
+    pid_msg[...] = jnp.broadcast_to(at_slot(partner), pid_msg.shape)
+    to_plan = pltpu.make_async_copy(plan, splan, tsem.at[1])
+    to_plan.start()
+    padded = lax.broadcasted_iota(jnp.int32, (batches, n * capp), 1)
+    home = target * capp + rank
+    pick = (padded == home[0:batches]) | (padded == home[batches:total])
+    pick_scr[...] = pick.astype(F32)
+    to_plan.wait()
 
     def fill(k):
         for r in range(cap):
-            e = src_ref[k, r]
-            own = ao_ref[e].astype(F32) * lo_ref[k, r].astype(F32)
-            mate = mate_ref[k, r]
-            other = ao_ref[mate].astype(F32) * lp_ref[k, r].astype(F32)
+            at = k * cap + r
+            e = splan[0, at]
+            own = ao_ref[e].astype(F32) * splan[2, at].astype(F32)
+            mate = splan[1, at]
+            other = ao_ref[mate].astype(F32) * splan[3, at].astype(F32)
             send_ao[k * cap + r, 0] = own.astype(BF16)
             send_ao[k * cap + r, 1] = other.astype(BF16)
 
     def pid_copy(d):
-        return copy(0, pidmsg_ref.at[peer(d)], recv_pid.at[me], d)
+        return copy(0, pid_msg, recv_pid.at[me], d)
 
     def pid_back(d):
-        return copy(0, pidmsg_ref.at[peer(d)], recv_pid.at[origin(d)], d)
+        return copy(0, pid_msg, recv_pid.at[origin(d)], d)
 
     def ao_copy(d):
         return copy(1, send_ao.at[mine(peer(d))], recv_ao.at[mine(me)], d)
@@ -113,7 +151,7 @@
     each(send_one)
     fill(me)
     recv_ao[mine(me)] = send_ao[mine(me)]
-    recv_pid[me] = pidmsg_ref[me]
+    recv_pid[me] = pid_msg[...]
 
     def den_body(c, carry):
         den[c] = den_ref[:, pl.ds(pl.multiple_of(c * width, width), width)]
@@ -138,9 +176,14 @@
     lax.fori_loop(0, batches // per, pre_body, 0)
 
     each(lambda d: pid_back(d).wait_recv())
-    pid_row = lax.fori_loop(
-        0, n, lambda i, a: a + recv_pid[i], jnp.zeros(recv_pid.shape[1:], jnp.int32)
-    )[0:1, :]
+    lists = jnp.max(recv_pid[...], axis=1)
+    lane = lax.broadcasted_iota(jnp.int32, (n, slots), 1)
+    base = lax.broadcasted_iota(jnp.int32, (n, slots), 0) * cap
+    gathered = jnp.zeros((n, slots), jnp.int32)
+    for r in range(cap):
+        mine_r = jnp.sum(jnp.where(lane == me * cap + r, lists, 0), axis=1, keepdims=True)
+        gathered = gathered + jnp.where(lane == base + r, mine_r, 0)
+    pid_row = jnp.sum(gathered, axis=0, keepdims=True)
     up = lax.broadcasted_iota(jnp.int32, (slots, slots), 0)
     across = lax.broadcasted_iota(jnp.int32, (slots, slots), 1)
     pid_col = jnp.sum(jnp.where(up == across, pid_row, 0), axis=1, keepdims=True)
@@ -193,10 +236,8 @@
     each(answer)
     each(lambda d: part_back(d).wait_recv())
 
-    slot_no = lax.broadcasted_iota(jnp.int32, (batches, n * capp), 1)
-    pick = (slot_no == slot_ref[:, 0:1]) | (slot_no == slot_ref[:, 1:2])
     rho_scr[...] = jnp.dot(
-        pick.astype(F32), ret[...].reshape(n * capp, 128), precision=highest,
+        pick_scr[...], ret[...].reshape(n * capp, 128), precision=highest,
         preferred_element_type=F32,
     )
     bias_base = features
@@ -253,11 +294,10 @@
         return carry
 
     lax.fori_loop(0, batches // per, body, 0)
-    batch_no = lax.broadcasted_iota(jnp.int32, (n * capp, batches), 1)
-    back = (batch_no == srcpad_ref[...]).astype(F32)
     send_w[:, capp:, :] = jnp.zeros((n, 8, 128), F32)
-    send_w[:, 0:capp, :] = jnp.dot(
-        back, pw_scr[...], precision=highest, preferred_element_type=F32
+    send_w[:, 0:capp, :] = lax.dot_general(
+        pick_scr[...], pw_scr[...], (((0,), (0,)), ((), ())), precision=highest,
+        preferred_element_type=F32,
     ).reshape(n, capp, 128)
     small_rows = out_row + 1
     for k in range(small_rows):
@@ -383,7 +423,6 @@
     w_out,
 ):
     n = lax.axis_size("wide")
-    me = lax.axis_index("wide")
     batches, entries, points, width = ao_values.shape
     blocks = density.shape[1] // width
     cap = max(2, (batches * entries + blocks - 1) // blocks)
@@ -394,25 +433,6 @@
     features = w_in.shape[0]
     total = batches * entries
     rows = batches * points
-    target = block_lists.reshape(-1)
-    ids = jnp.arange(total, dtype=jnp.int32)
-    earlier = (target[:, None] == target[None, :]) & (ids[None, :] < ids[:, None])
-    rank = jnp.sum(earlier.astype(jnp.int32), axis=1)
-    slot_of = target * cap + rank
-    table = slot_of[None, :] == jnp.arange(slots, dtype=jnp.int32)[:, None]
-    live = (jnp.arange(entries)[None, :] < counts[:, None]).astype(jnp.int32)
-
-    def at_slot(values):
-        return jnp.sum(jnp.where(table, values.reshape(-1)[None, :], 0), axis=1).reshape(n, cap)
-
-    source = at_slot(ids)
-    partner = at_slot(jnp.flip(block_lists, 1))
-    live_own = at_slot(live)
-    live_other = at_slot(jnp.flip(live, 1))
-    filled = jnp.any(table, axis=1).reshape(n, cap)
-    lane = jnp.arange(slots, dtype=jnp.int32)
-    spread = jnp.where(lane[None, :] // cap == me, jnp.tile(partner, (1, n)), 0)
-    pid_msg = jnp.broadcast_to(spread[:, None, :], (n, 8, slots))
     feat = jnp.concatenate(
         [
             jnp.zeros((1, rows), F32),
@@ -420,9 +440,6 @@
         ],
         axis=0,
     )
-    slot_pad = (target * capp + rank).reshape(batches, entries)
-    src_pad = jnp.where(filled, source // entries, -1)
-    src_pad = jnp.pad(src_pad, ((0, 0), (0, capp - cap)), constant_values=-1).reshape(n * capp, 1)
     weight_rows = layers * hidden
     chunk_rows = (-(-weight_rows // n) + 15) // 16 * 16
     while weight_rows % chunk_rows:
@@ -438,13 +455,17 @@
             jax.ShapeDtypeStruct((layers + 1, hidden), F32),
             jax.ShapeDtypeStruct((1, hidden), F32),
         ),
-        in_specs=[SMEM] * 4 + [VMEM] * 11,
+        in_specs=[VMEM] * 10,
         out_specs=(VMEM,) * 5,
         scratch_shapes=[
             vm((slots, 2, points, width), BF16),
             vm((slots, 2, points, width), BF16),
+            vm((8, slots), jnp.int32),
             vm((n, 8, slots), jnp.int32),
             vm((8, slots), jnp.int32),
+            vm((8, slots), jnp.int32),
+            pltpu.SMEM((8, slots), jnp.int32),
+            vm((batches, n * capp), F32),
             pltpu.SMEM((8, slots), jnp.int32),
             vm((n, capp, 128), F32),
             vm((n, capp, 128), F32),
@@ -466,14 +487,13 @@
             vm((blocks, width, width), BF16),
             pltpu.SemaphoreType.DMA((7, n)),
             pltpu.SemaphoreType.DMA((7, n)),
-            pltpu.SemaphoreType.DMA((1,)),
+            pltpu.SemaphoreType.DMA((2,)),
         ],
         compiler_params=pltpu.CompilerParams(
             vmem_limit_bytes=56 * 1024 * 1024, collective_id=0, has_side_effects=True
         ),
     )(
-        source, source ^ 1, live_own, live_other, pid_msg, ao_values.reshape(total, points, width), density,
-        slot_pad, src_pad, feat, quad_weights, w_in, biases, w_layers, w_out[None, :],
+        block_lists, counts[None, :], ao_values.reshape(total, points, width), density, feat, quad_weights, w_in, biases, w_layers, w_out[None, :],
     )
     return (potential, gw.reshape(layers, hidden, hidden), gin, gbias, gout.reshape(hidden))
 

time: 111 us -> 105 us (0.946)
  local copies, waits for them, and re-layouts: 11.9 us -> 8.72 us
  other arithmetic: 2.48 us -> 0 us
    reshape x4 -> x0, local copies, waits for them, and re-layouts: 1.58 us -> none  [the longest x3 1.44 us: at_slot(): jnp.sum(jnp.where(table, values.reshape(-1)[None, :], 0), axis=1)]
    unnamed x25 -> x19, local copies, waits for them, and re-layouts: 7.35 us -> 6.83 us
where the time goes in v3:
time: 105 us; the launch traced here: 103 us
  Pallas kernels  93.7 us (89%)
  local copies, waits for them, and re-layouts  8.72 us (8%)
    pallas_call x1, Pallas kernels, shards(): pl.pallas_call(functools.partial(fused_kernel, cap, chunk_rows), out_shap...  93.7 us
    unnamed x19, local copies, waits for them, and re-layouts  6.83 us

profile of v3, /device:TPU:0, one launch (start us, length us, event | category | flops | bytes accessed | tf_op | source)
XLA Modules:
  0.0 103.1 jit_solution(11392631831036824191)
XLA Ops:
  0.6 0.0 copy-start.4
  0.6 0.7 copy-done.4
  1.3 0.0 copy-start.1
  1.3 0.7 copy.19.list_ref
  2.0 0.0 copy-done.1
  2.0 0.7 copy.20.quad_ref
  2.7 1.1 %copy.18 = f32[10,64,32]{2,1,0:T(8,128)S(1)} copy(f32[10,64,32]{1,2,0:T(8,128)} %bitcast.8) | data formatting | bytes 163840 | tf_op jit(solution)/shard_map/transpose | solution.py:439
  3.8 0.2 reshape.23
  4.0 0.7 concatenate.3.feat_ref
  4.6 93.7 %shard_map.137 = (bf16[128,2048]{1,0:T(8,128)(2,1)}, f32[768,256]{1,0:T(8,128)}, f32[11,256]{1,0:T(8,128)}, f32[4,256]{1,0:T(4,128)}, f32[1,256]{1,0:T(1,128)}) custom-call(s32[64,2]{1,0:T(8,128)} %copy.19.list_ref, s32[1,64]{1,0:T(1,128)} %bitcast.11, bf16[128,32,128]{2,1,0:T(8,128)(2,1)} %bitcast.6, bf16[128,2048]{1,0:T(8,128)(2,1)} %den_ref.1, ...), custom_call_target="tpu_custom_call" | custom-call | tf_op jit(solution)/shard_map/pallas_call | solution.py:449
  98.3 0.0 copy-start
  98.4 2.0 %copy.26 = bf16[128,2048]{1,0:T(8,128)(2,1)} copy(bf16[128,2048]{1,0:T(8,128)(2,1)} %get-tuple-element.20) | data formatting | bytes 1048576
  100.3 0.0 copy-done
  100.3 0.0 copy-start.2
  100.3 0.9 copy.27
  101.2 0.0 copy-done.2
  101.2 0.0 copy-start.3
  101.2 0.6 copy.28
  101.8 0.1 copy-done.3
  101.9 0.0 copy-start.5
  101.9 0.6 copy.29
  102.5 0.1 copy-done.5
  102.5 0.6 copy.30
Async XLA Ops:
  0.6 0.7 copy-start.4
  1.3 0.7 copy-start.1
  98.3 2.0 %copy-start = (f32[768,256]{1,0:T(8,128)S(1)}, f32[768,256]{1,0:T(8,128)}, u32[]{:S(2)}) copy-start(f32[768,256]{1,0:T(8,128)} %get-tuple-element.11) | copy-start | bytes 2359300
  100.3 0.9 copy-start.2
  101.2 0.7 copy-start.3
  101.9 0.7 copy-start.5

commit v4 on v3

--- a/solution.py
+++ b/solution.py
@@ -12,7 +12,6 @@
 BF16 = jnp.bfloat16
 CHUNK = 512
 VMEM = pl.BlockSpec(memory_space=pltpu.VMEM)
-SMEM = pl.BlockSpec(memory_space=pltpu.SMEM)
 
 
 def up8(x):
@@ -30,20 +29,23 @@
 
 
 def fused_kernel(
-    cap, chunk_rows,
+    cap, rows_each,
     list_ref, count_ref, ao_ref, den_ref, feat_ref, quad_ref,
     win_ref, bias_ref, wl_ref, wout_ref,
     pot_ref, gw_ref, gin_ref, gbias_ref, gout_ref,
-    send_ao, recv_ao, pid_msg, recv_pid, table, plan, splan, pick_scr, stable, send_part, ret, pre_scr, rho_scr, quad_scr, pw_scr,
-    small, grads, send_w, recv_w, send_g, recv_g, send_a, recv_a, send_s, recv_s, prefix, den,
-    ssem, rsem, tsem,
+    send_ao, recv_ao, pid_msg, recv_pid, table, plan, splan, pick_scr, stable, send_part, ret, pre_scr,
+    rho_scr, quad_col_scr, pw_scr, feat_hi, feat_lo, acts_scr, round_scr,
+    small, grads, send_w, recv_w, send_m, recv_m, send_g, recv_g, send_a, recv_a, send_s, recv_s,
+    prefix, den,
+    ssem, rsem, tsem, dsem,
 ):
     n = send_part.shape[0]
     points, width = ao_ref.shape[1:]
-    batches = quad_ref.shape[0]
+    batches = quad_ref.shape[1]
+    rows = points * batches
     hidden = wout_ref.shape[1]
     layers = wl_ref.shape[0]
-    features = feat_ref.shape[0]
+    features = win_ref.shape[0]
     halves = hidden // 128
     slots = n * cap
     capp = send_part.shape[1]
@@ -81,19 +83,38 @@
         )
 
     each(greet)
+
+    def den_copy(c):
+        return pltpu.make_async_copy(
+            den_ref.at[:, pl.ds(pl.multiple_of(c * width, width), width)], den.at[c], dsem.at[c]
+        )
+
+    def den_start(c, carry):
+        den_copy(c).start()
+        return carry
+
+    def den_wait(c, carry):
+        den_copy(c).wait()
+        return carry
+
+    lax.fori_loop(0, blocks, den_start, 0)
     total = batches * 2
     up = lax.broadcasted_iota(jnp.int32, (total, total), 0)
     across = lax.broadcasted_iota(jnp.int32, (total, total), 1)
-    first_ids = list_ref[:, 0:1]
-    second_ids = list_ref[:, 1:2]
+    square = (batches, batches)
+    same = lax.broadcasted_iota(jnp.int32, square, 0) == lax.broadcasted_iota(jnp.int32, square, 1)
+
+    def stand(row):
+        return jnp.sum(jnp.where(same, row, 0), axis=1, keepdims=True)
+
+    first_ids = stand(list_ref[0:1, :])
+    second_ids = stand(list_ref[1:2, :])
     target = jnp.concatenate([first_ids, second_ids], axis=0)
     partner = jnp.concatenate([second_ids, first_ids], axis=0)
     target_row = jnp.sum(jnp.where(up == across, target, 0), axis=0, keepdims=True)
     earlier = (target_row == target) & (across < up)
     rank = jnp.sum(earlier.astype(jnp.int32), axis=1, keepdims=True)
-    square = (batches, batches)
-    same = lax.broadcasted_iota(jnp.int32, square, 0) == lax.broadcasted_iota(jnp.int32, square, 1)
-    used = jnp.sum(jnp.where(same, count_ref[...], 0), axis=1, keepdims=True)
+    used = stand(count_ref[...])
     used = jnp.concatenate([used, used], axis=0)
     entry = lax.broadcasted_iota(jnp.int32, (total, 1), 0)
     second = (entry >= batches).astype(jnp.int32)
@@ -153,27 +174,33 @@
     recv_ao[mine(me)] = send_ao[mine(me)]
     recv_pid[me] = pid_msg[...]
 
-    def den_body(c, carry):
-        den[c] = den_ref[:, pl.ds(pl.multiple_of(c * width, width), width)]
-        return carry
-
-    lax.fori_loop(0, blocks, den_body, 0)
-    per = CHUNK // points
-    quad_scr[...] = jnp.zeros_like(quad_scr)
-    quad_scr[:, 0:points] = quad_ref[...]
+    per = CHUNK // batches
+    chunks = rows // CHUNK
     grads[...] = jnp.zeros_like(grads)
     small[...] = jnp.zeros_like(small)
-
-    def pre_body(k, carry):
-        row = pl.multiple_of(k * CHUNK, CHUNK)
+    pw_scr[...] = jnp.zeros_like(pw_scr)
+    feat_hi[...] = jnp.zeros_like(feat_hi)
+    feat_lo[...] = jnp.zeros_like(feat_lo)
+    wide_eye = eye_mask(batches)[:, 0:batches]
+
+    def as_col(block):
+        spread = jnp.where(wide_eye[None], block[:, None, :], 0.0)
+        return jnp.sum(spread, axis=2, keepdims=True).reshape(CHUNK, 1)
+
+    for k in range(chunks):
+        at = k * CHUNK
+        block = jnp.concatenate(
+            [feat_ref[:, p, :] for p in range(k * per, (k + 1) * per)], axis=1
+        )
         part = lax.dot_general(
-            feat_ref[:, pl.ds(row, CHUNK)], win_ref[...], (((0,), (0,)), ((), ())),
-            precision=highest, preferred_element_type=F32,
-        )
-        pre_scr[pl.ds(row, CHUNK), :] = part + bias_ref[0:1, :]
-        return carry
-
-    lax.fori_loop(0, batches // per, pre_body, 0)
+            block, win_ref[1:features, :], (((0,), (0,)), ((), ())), precision=highest,
+            preferred_element_type=F32,
+        )
+        pre_scr[at : at + CHUNK, :] = part + bias_ref[0:1, :]
+        quad_col_scr[at : at + CHUNK, :] = as_col(quad_ref[k * per : (k + 1) * per, :])
+        hi = block.astype(BF16)
+        feat_hi[0 : features - 1, at : at + CHUNK] = hi
+        feat_lo[0 : features - 1, at : at + CHUNK] = (block - hi.astype(F32)).astype(BF16)
 
     each(lambda d: pid_back(d).wait_recv())
     lists = jnp.max(recv_pid[...], axis=1)
@@ -202,6 +229,7 @@
     to_scalar.start()
     to_scalar.wait()
 
+    lax.fori_loop(0, blocks, den_wait, 0)
     own = den[me]
 
     def shares(i):
@@ -236,113 +264,173 @@
     each(answer)
     each(lambda d: part_back(d).wait_recv())
 
-    rho_scr[...] = jnp.dot(
-        pick_scr[...], ret[...].reshape(n * capp, 128), precision=highest,
-        preferred_element_type=F32,
+    rho = lax.dot_general(
+        ret[...].reshape(n * capp, 128), pick_scr[...], (((0,), (1,)), ((), ())),
+        precision=highest, preferred_element_type=F32,
     )
+    rho_scr[...] = rho[0:points, :]
     bias_base = features
     out_row = bias_base + layers + 1
-
-    def as_col(block):
-        spread = jnp.where(eye[None], block[:, None, :], 0.0)
-        return jnp.sum(spread, axis=2, keepdims=True).reshape(CHUNK, 1)
-
-    def body(k, carry):
+    small_rows = out_row + 1
+    holders = hidden // rows_each
+
+    def g_copy(l, d):
+        return copy(6 + l, send_g.at[l, lax.rem(peer(d), holders)], recv_g.at[l, me], d)
+
+    def g_back(l, d):
+        return copy(6 + l, send_g.at[l, lax.rem(peer(d), holders)], recv_g.at[l, origin(d)], d)
+
+    def a_copy(l, d):
+        return copy(6 + layers + l, send_a.at[l], recv_a.at[l, me], d)
+
+    def a_back(l, d):
+        return copy(6 + layers + l, send_a.at[l], recv_a.at[l, origin(d)], d)
+
+    def send_grads(l):
+        for k in range(holders):
+            at = k * rows_each
+            send_g[l, k] = grads[l, at : at + rows_each, :].astype(BF16)
+        each(lambda d: g_copy(l, d).start())
+
+    def share_grads(l):
+        each(lambda d: g_back(l, d).wait_recv())
+        recv_g[l, me] = jnp.zeros((rows_each, hidden), BF16)
+        at = pl.multiple_of(lax.rem(me, holders) * rows_each, 16)
+        added = lax.fori_loop(
+            0, n, lambda i, a: a + recv_g[l, i].astype(F32), grads[l, pl.ds(at, rows_each), :]
+        )
+        send_a[l] = added.astype(BF16)
+        each(lambda d: a_copy(l, d).start())
+        recv_a[l, me] = added.astype(BF16)
+
+    def step_back(l, row, grad):
+        after = acts_scr[l + 1, pl.ds(row, CHUNK), :].astype(F32)
+        grad = grad * (1.0 - after * after)
+        b = bias_base + l + 1
+        small[b : b + 1, :] += jnp.sum(grad, axis=0, keepdims=True)
+        return grad.astype(BF16)
+
+    def add_weight(l, row, rounded):
+        grads[l] += col_dot(acts_scr[l, pl.ds(row, CHUNK), :], rounded)
+
+    def through(l, rounded):
+        return lax.dot_general(
+            rounded, wl_ref[l], (((1,), (1,)), ((), ())), preferred_element_type=F32
+        )
+
+    def forward(k, carry):
+        row = pl.multiple_of(k * CHUNK, CHUNK)
+        rho_col = as_col(rho_scr[pl.ds(pl.multiple_of(k * per, per), per), :])
+        act = jnp.tanh(pre_scr[pl.ds(row, CHUNK), :] + rho_col * win_ref[0:1, :]).astype(BF16)
+        acts_scr[0, pl.ds(row, CHUNK), :] = act
+        for l in range(layers):
+            inner = jnp.dot(act, wl_ref[l], preferred_element_type=F32)
+            act = jnp.tanh(inner + bias_ref[l + 1 : l + 2, :]).astype(BF16)
+            acts_scr[l + 1, pl.ds(row, CHUNK), :] = act
+        top = act.astype(F32)
+        score = jnp.sum(top * wout_ref[...], axis=1, keepdims=True)
+        enhance = 2.0 * jax.nn.sigmoid(score)
+        weighted = quad_col_scr[pl.ds(row, CHUNK), :] * enhance
+        quad_col_scr[pl.ds(row, CHUNK), :] = weighted
+        grad_score = weighted * rho_col * (1.0 - 0.5 * enhance)
+        small[out_row : out_row + 1, :] += jnp.sum(grad_score * top, axis=0, keepdims=True)
+        last = layers - 1
+        rounded = step_back(last, row, grad_score * wout_ref[...])
+        add_weight(last, row, rounded)
+        pre_scr[pl.ds(row, CHUNK), :] = through(last, rounded)
+        return carry
+
+    lax.fori_loop(0, chunks, forward, 0)
+    send_grads(layers - 1)
+    for l in range(layers - 2, 0, -1):
+
+        def middle(k, carry):
+            row = pl.multiple_of(k * CHUNK, CHUNK)
+            rounded = step_back(l, row, pre_scr[pl.ds(row, CHUNK), :])
+            add_weight(l, row, rounded)
+            pre_scr[pl.ds(row, CHUNK), :] = through(l, rounded)
+            return carry
+
+        lax.fori_loop(0, chunks, middle, 0)
+        send_grads(l)
+
+    def bottom(k, carry):
         at = pl.multiple_of(k * per, per)
         row = pl.multiple_of(k * CHUNK, CHUNK)
-        rho_col = as_col(rho_scr[pl.ds(at, per), :])
-        quad_col = as_col(quad_scr[pl.ds(at, per), :])
-        pre = pre_scr[pl.ds(row, CHUNK), :] + rho_col * win_ref[0:1, :]
-        acts = [jnp.tanh(pre).astype(BF16)]
-        for l in range(layers):
-            inner = jnp.dot(acts[-1], wl_ref[l], preferred_element_type=F32)
-            acts.append(jnp.tanh(inner + bias_ref[l + 1 : l + 2, :]).astype(BF16))
-        top = acts[-1].astype(F32)
-        score = jnp.sum(top * wout_ref[...], axis=1, keepdims=True)
-        enhance = 2.0 * jax.nn.sigmoid(score)
-        grad_score = quad_col * rho_col * enhance * (1.0 - 0.5 * enhance)
-        small[out_row : out_row + 1, :] += jnp.sum(grad_score * top, axis=0, keepdims=True)
-        grad = grad_score * wout_ref[...]
-        for l in reversed(range(layers)):
-            after = acts[l + 1].astype(F32)
-            grad = grad * (1.0 - after * after)
-            rounded = grad.astype(BF16)
-            grads[l * hidden : (l + 1) * hidden, :] += col_dot(acts[l], rounded)
-            b = bias_base + l + 1
-            small[b : b + 1, :] += jnp.sum(grad, axis=0, keepdims=True)
-            grad = lax.dot_general(
-                rounded, wl_ref[l], (((1,), (1,)), ((), ())), preferred_element_type=F32
-            )
-        first = acts[0].astype(F32)
+        rounded = step_back(0, row, pre_scr[pl.ds(row, CHUNK), :])
+        round_scr[pl.ds(row, CHUNK), :] = rounded
+        grad = through(0, rounded)
+        first = acts_scr[0, pl.ds(row, CHUNK), :].astype(F32)
         grad = grad * (1.0 - first * first)
+        pre_scr[pl.ds(row, CHUNK), :] = grad
+        grad_rho = jnp.sum(grad * win_ref[0:1, :], axis=1, keepdims=True)
+        weight = (quad_col_scr[pl.ds(row, CHUNK), :] + grad_rho).reshape(per, batches, 1)
+        pw_scr[pl.ds(at, per), 0:batches] = jnp.sum(jnp.where(wide_eye[None], weight, 0.0), axis=1)
+        return carry
+
+    lax.fori_loop(0, chunks, bottom, 0)
+    send_w[...] = lax.dot_general(
+        pick_scr[...], pw_scr[:, 0:batches], (((0,), (1,)), ((), ())), precision=highest,
+        preferred_element_type=F32,
+    ).reshape(n, capp, 128)
+
+    def w_copy(d):
+        return copy(3, send_w.at[peer(d)], recv_w.at[me], d)
+
+    def w_back(d):
+        return copy(3, send_w.at[peer(d)], recv_w.at[origin(d)], d)
+
+    def m_copy(d):
+        return copy(4, send_m.at[peer(d)], recv_m.at[me], d)
+
+    def m_back(d):
+        return copy(4, send_m.at[peer(d)], recv_m.at[origin(d)], d)
+
+    def s_copy(d):
+        return copy(5, send_s, recv_s.at[me], d)
+
+    def s_back(d):
+        return copy(5, send_s, recv_s.at[origin(d)], d)
+
+    each(lambda d: w_copy(d).start())
+    recv_w[me] = send_w[me]
+
+    def late(k, carry):
+        row = pl.multiple_of(k * CHUNK, CHUNK)
+        add_weight(0, row, round_scr[pl.ds(row, CHUNK), :])
+        return carry
+
+    lax.fori_loop(0, chunks, late, 0)
+    send_grads(0)
+
+    def late_input(k, carry):
+        row = pl.multiple_of(k * CHUNK, CHUNK)
+        rho_col = as_col(rho_scr[pl.ds(pl.multiple_of(k * per, per), per), :])
+        grad = pre_scr[pl.ds(row, CHUNK), :]
         small[bias_base : bias_base + 1, :] += jnp.sum(grad, axis=0, keepdims=True)
         small[0:1, :] += jnp.sum(grad * rho_col, axis=0, keepdims=True)
         hi = grad.astype(BF16)
         lo = (grad - hi.astype(F32)).astype(BF16)
-        feat = feat_ref[:, pl.ds(row, CHUNK)]
-        fhi = feat.astype(BF16)
-        flo = (feat - fhi.astype(F32)).astype(BF16)
+        fhi = feat_hi[:, pl.ds(row, CHUNK)]
+        flo = feat_lo[:, pl.ds(row, CHUNK)]
         term = (
             jnp.dot(fhi, hi, preferred_element_type=F32)
             + jnp.dot(fhi, lo, preferred_element_type=F32)
             + jnp.dot(flo, hi, preferred_element_type=F32)
         )
-        small[1:features, :] += term[1:features]
-        grad_rho = jnp.sum(grad * win_ref[0:1, :], axis=1, keepdims=True)
-        weight = (quad_col * enhance + grad_rho).reshape(per, points, 1)
-        pw_scr[pl.ds(at, per), :] = jnp.sum(jnp.where(eye[None], weight, 0.0), axis=1)
+        small[1:features, :] += term[0 : features - 1]
         return carry
 
-    lax.fori_loop(0, batches // per, body, 0)
-    send_w[:, capp:, :] = jnp.zeros((n, 8, 128), F32)
-    send_w[:, 0:capp, :] = lax.dot_general(
-        pick_scr[...], pw_scr[...], (((0,), (0,)), ((), ())), precision=highest,
-        preferred_element_type=F32,
-    ).reshape(n, capp, 128)
-    small_rows = out_row + 1
+    lax.fori_loop(0, chunks, late_input, 0)
+    send_m[...] = jnp.zeros_like(send_m)
     for k in range(small_rows):
         for h in range(halves):
-            send_w[k, capp + h : capp + h + 1, :] = small[k : k + 1, h * 128 : (h + 1) * 128]
-
-    def w_copy(d):
-        return copy(3, send_w.at[peer(d)], recv_w.at[me], d)
-
-    def w_back(d):
-        return copy(3, send_w.at[peer(d)], recv_w.at[origin(d)], d)
-
-    def g_copy(d):
-        return copy(4, send_g.at[peer(d)], recv_g.at[me], d)
-
-    def g_back(d):
-        return copy(4, send_g.at[peer(d)], recv_g.at[origin(d)], d)
-
-    def a_copy(d):
-        return copy(5, send_a, recv_a.at[me], d)
-
-    def a_back(d):
-        return copy(5, send_a, recv_a.at[origin(d)], d)
-
-    def s_copy(d):
-        return copy(6, send_s, recv_s.at[me], d)
-
-    def s_back(d):
-        return copy(6, send_s, recv_s.at[origin(d)], d)
-
-    each(lambda d: w_copy(d).start())
-
-    def send_grad(d):
-        k = peer(d)
-        at = pl.multiple_of(k * chunk_rows, 16)
-        send_g[k] = grads[pl.ds(at, chunk_rows), :].astype(BF16)
-        g_copy(d).start()
-
-    each(send_grad)
-    recv_w[me] = send_w[me]
+            send_m[k, h : h + 1, :] = small[k : k + 1, h * 128 : (h + 1) * 128]
+    each(lambda d: m_copy(d).start())
+    recv_m[me] = send_m[me]
+    for l in range(layers - 1, 0, -1):
+        share_grads(l)
     each(lambda d: w_back(d).wait_recv())
-    send_s[...] = lax.fori_loop(
-        0, n, lambda i, a: a + recv_w[i, capp:, :], jnp.zeros((8, 128), F32)
-    )
-    each(lambda d: s_copy(d).start())
 
     def own_body(i, acc):
         w = recv_w[i]
@@ -358,6 +446,10 @@
 
     each(lambda d: ao_copy(d).wait_send())
     own_sum = lax.fori_loop(0, n, own_body, jnp.zeros((width, width), F32))
+    share_grads(0)
+    each(lambda d: m_back(d).wait_recv())
+    send_s[...] = lax.fori_loop(0, n, lambda i, a: a + recv_m[i], jnp.zeros((8, 128), F32))
+    each(lambda d: s_copy(d).start())
     group = 8
 
     def sorted_body(g, acc):
@@ -371,14 +463,6 @@
 
     lax.fori_loop(0, slots // group, sorted_body, jnp.zeros((width, width), F32))
 
-    at = pl.multiple_of(me * chunk_rows, 16)
-    each(lambda d: g_back(d).wait_recv())
-    total = grads[pl.ds(at, chunk_rows), :]
-    recv_g[me] = jnp.zeros(recv_g.shape[1:], BF16)
-    total = lax.fori_loop(0, n, lambda i, a: a + recv_g[i].astype(F32), total)
-    send_a[...] = total.astype(BF16)
-    each(lambda d: a_copy(d).start())
-
     def out_body(c, carry):
         end = stable[3, c]
         value = prefix[end] * stable[4, c].astype(F32)
@@ -387,7 +471,6 @@
         return carry
 
     lax.fori_loop(0, blocks, out_body, 0)
-    recv_a[me] = send_a[...]
     recv_s[me] = send_s[...]
     each(lambda d: s_back(d).wait_recv())
     for k in range(small_rows):
@@ -398,22 +481,25 @@
             gbias_ref[k - features : k - features + 1, :] = row
         else:
             gout_ref[...] = row
-    each(lambda d: a_back(d).wait_recv())
-
-    def gw_body(k, carry):
-        at = pl.multiple_of(k * chunk_rows, 16)
-        gw_ref[pl.ds(at, chunk_rows), :] = recv_a[k].astype(F32)
-        return carry
-
-    lax.fori_loop(0, layers * hidden // chunk_rows, gw_body, 0)
+    for l in range(layers - 1, -1, -1):
+        each(lambda d: a_back(l, d).wait_recv())
+
+        def gw_body(k, carry):
+            at = pl.multiple_of(k * rows_each, 16)
+            gw_ref[l, pl.ds(at, rows_each), :] = recv_a[l, k].astype(F32)
+            return carry
+
+        lax.fori_loop(0, holders, gw_body, 0)
 
     def drain(d):
         pid_copy(d).wait_send()
         part_copy(d).wait_send()
         w_copy(d).wait_send()
-        g_copy(d).wait_send()
-        a_copy(d).wait_send()
+        m_copy(d).wait_send()
         s_copy(d).wait_send()
+        for l in range(layers):
+            g_copy(l, d).wait_send()
+            a_copy(l, d).wait_send()
 
     each(drain)
 
@@ -433,29 +519,21 @@
     features = w_in.shape[0]
     total = batches * entries
     rows = batches * points
-    feat = jnp.concatenate(
-        [
-            jnp.zeros((1, rows), F32),
-            other_features.transpose(1, 0, 2).reshape(features - 1, rows),
-        ],
-        axis=0,
-    )
-    weight_rows = layers * hidden
-    chunk_rows = (-(-weight_rows // n) + 15) // 16 * 16
-    while weight_rows % chunk_rows:
-        chunk_rows += 16
+    rows_each = (-(-hidden // n) + 15) // 16 * 16
+    while hidden % rows_each:
+        rows_each += 16
     small_rows = up8(features + layers + 2)
     vm = pltpu.VMEM
     potential, gw, gin, gbias, gout = pl.pallas_call(
-        functools.partial(fused_kernel, cap, chunk_rows),
+        functools.partial(fused_kernel, cap, rows_each),
         out_shape=(
             jax.ShapeDtypeStruct(density.shape, density.dtype),
-            jax.ShapeDtypeStruct((weight_rows, hidden), F32),
+            jax.ShapeDtypeStruct((layers, hidden, hidden), F32),
             jax.ShapeDtypeStruct((features, hidden), F32),
             jax.ShapeDtypeStruct((layers + 1, hidden), F32),
             jax.ShapeDtypeStruct((1, hidden), F32),
         ),
-        in_specs=[VMEM] * 10,
+        in_specs=[VMEM] * 3 + [pl.BlockSpec(memory_space=pl.ANY)] + [VMEM] * 6,
         out_specs=(VMEM,) * 5,
         scratch_shapes=[
             vm((slots, 2, points, width), BF16),
@@ -470,32 +548,39 @@
             vm((n, capp, 128), F32),
             vm((n, capp, 128), F32),
             vm((rows, hidden), F32),
-            vm((batches, 128), F32),
-            vm((batches, 128), F32),
-            vm((batches, 128), F32),
+            vm((points, batches), F32),
+            vm((rows, 1), F32),
+            vm((128, 128), F32),
+            vm((16, rows), BF16),
+            vm((16, rows), BF16),
+            vm((layers + 1, rows, hidden), BF16),
+            vm((rows, hidden), BF16),
             vm((small_rows, hidden), F32),
-            vm((n * chunk_rows, hidden), F32),
-            vm((n, capp + 8, 128), F32),
-            vm((n, capp + 8, 128), F32),
-            vm((n, chunk_rows, hidden), BF16),
-            vm((n, chunk_rows, hidden), BF16),
-            vm((chunk_rows, hidden), BF16),
-            vm((n, chunk_rows, hidden), BF16),
+            vm((layers, hidden, hidden), F32),
+            vm((n, capp, 128), F32),
+            vm((n, capp, 128), F32),
+            vm((n, 8, 128), F32),
+            vm((n, 8, 128), F32),
+            vm((layers, hidden // rows_each, rows_each, hidden), BF16),
+            vm((layers, n, rows_each, hidden), BF16),
+            vm((layers, rows_each, hidden), BF16),
+            vm((layers, n, rows_each, hidden), BF16),
             vm((8, 128), F32),
             vm((n, 8, 128), F32),
             vm((slots, width, width), F32),
             vm((blocks, width, width), BF16),
-            pltpu.SemaphoreType.DMA((7, n)),
-            pltpu.SemaphoreType.DMA((7, n)),
+            pltpu.SemaphoreType.DMA((6 + 2 * layers, n)),
+            pltpu.SemaphoreType.DMA((6 + 2 * layers, n)),
             pltpu.SemaphoreType.DMA((2,)),
+            pltpu.SemaphoreType.DMA((blocks,)),
         ],
         compiler_params=pltpu.CompilerParams(
-            vmem_limit_bytes=56 * 1024 * 1024, collective_id=0, has_side_effects=True
+            vmem_limit_bytes=59 * 1024 * 1024, collective_id=0, has_side_effects=True
         ),
     )(
-        block_lists, counts[None, :], ao_values.reshape(total, points, width), density, feat, quad_weights, w_in, biases, w_layers, w_out[None, :],
+        block_lists.T, counts[None, :], ao_values.reshape(total, points, width), density, other_features.transpose(1, 2, 0), quad_weights.T, w_in, biases, w_layers, w_out[None, :],
     )
-    return (potential, gw.reshape(layers, hidden, hidden), gin, gbias, gout.reshape(hidden))
+    return (potential, gw, gin, gbias, gout.reshape(hidden))
 
 
 def solution(mesh):

time: 105 us -> 98.8 us (0.941); the launches traced: 103 us -> 98.5 us
  local copies, waits for them, and re-layouts: 8.72 us -> 4.75 us
    unnamed x19 -> x13, local copies, waits for them, and re-layouts: 6.83 us -> 4.75 us
    transpose x1 -> x0, local copies, waits for them, and re-layouts: 1.07 us -> none  [shards(): other_features.transpose(1, 0, 2).reshape(features - 1, rows)]
where the time goes in v4:
time: 98.8 us; the launch traced here: 98.5 us
  Pallas kernels  93.1 us (94%)
  local copies, waits for them, and re-layouts  4.75 us (5%)
    pallas_call x1, Pallas kernels, shards(): pl.pallas_call(functools.partial(fused_kernel, cap, rows_each), out_shape...  93.1 us
    unnamed x13, local copies, waits for them, and re-layouts  4.75 us

profile of v4, /device:TPU:0, one launch (start us, length us, event | category | flops | bytes accessed | tf_op | source)
XLA Modules:
  0.0 98.5 jit_solution(13077022440171591646)
XLA Ops:
  0.6 93.1 %shard_map.137 = (bf16[128,2048]{1,0:T(8,128)(2,1)}, f32[3,256,256]{2,1,0:T(8,128)}, f32[11,256]{1,0:T(8,128)}, f32[4,256]{1,0:T(4,128)}, f32[1,256]{1,0:T(1,128)}) custom-call(s32[2,64]{1,0:T(2,128)} %bitcast.10, s32[1,64]{1,0:T(1,128)} %bitcast.13, bf16[128,32,128]{2,1,0:T(8,128)(2,1)} %bitcast.7, bf16[128,2048]{1,0:T(8,128)(2,1)} %den_ref.1, ...), custom_call_target="tpu_custom_call" | custom-call | tf_op jit(solution)/shard_map/pallas_call | solution.py:527
  93.8 0.0 copy-start
  93.8 2.0 %copy.20 = bf16[128,2048]{1,0:T(8,128)(2,1)} copy(bf16[128,2048]{1,0:T(8,128)(2,1)} %get-tuple-element.20) | data formatting | bytes 1048576
  95.7 0.0 copy-done
  95.8 0.0 copy-start.1
  95.8 0.9 copy.21
  96.6 0.0 copy-done.1
  96.6 0.0 copy-start.2
  96.6 0.6 copy.22
  97.2 0.1 copy-done.2
  97.3 0.0 copy-start.3
  97.3 0.6 copy.23
  97.9 0.1 copy-done.3
  98.0 0.6 copy.24
Async XLA Ops:
  93.8 2.0 %copy-start = (f32[3,256,256]{2,1,0:T(8,128)S(1)}, f32[3,256,256]{2,1,0:T(8,128)}, u32[]{:S(2)}) copy-start(f32[3,256,256]{2,1,0:T(8,128)} %get-tuple-element.21) | copy-start | bytes 2359300
  95.8 0.9 copy-start.1
  96.6 0.7 copy-start.2
  97.3 0.7 copy-start.3

commit v5 on v4

--- a/solution.py
+++ b/solution.py
@@ -10,7 +10,7 @@
 highest = lax.Precision.HIGHEST
 F32 = jnp.float32
 BF16 = jnp.bfloat16
-CHUNK = 512
+CHUNK = 1024
 VMEM = pl.BlockSpec(memory_space=pltpu.VMEM)
 
 
@@ -162,15 +162,15 @@
     def ao_back(d):
         return copy(1, send_ao.at[mine(peer(d))], recv_ao.at[mine(origin(d))], d)
 
+    def fill_body(k, carry):
+        fill(k)
+        return carry
+
+    lax.fori_loop(0, n, fill_body, 0)
     pl.semaphore_wait(barrier, n - 1)
     each(lambda d: pid_copy(d).start())
 
-    def send_one(d):
-        fill(peer(d))
-        ao_copy(d).start()
-
-    each(send_one)
-    fill(me)
+    each(lambda d: ao_copy(d).start())
     recv_ao[mine(me)] = send_ao[mine(me)]
     recv_pid[me] = pid_msg[...]
 

time: 98.8 us -> 98.2 us (level)
  no operation moved by 1% of the time
where the time goes in v5:
time: 98.2 us; the launch traced here: 98 us
  Pallas kernels  92.6 us (94%)
  local copies, waits for them, and re-layouts  4.75 us (5%)
    pallas_call x1, Pallas kernels, shards(): pl.pallas_call(functools.partial(fused_kernel, cap, rows_each), out_shape...  92.6 us
    unnamed x13, local copies, waits for them, and re-layouts  4.75 us

profile of v5, /device:TPU:0, one launch (start us, length us, event | category | flops | bytes accessed | tf_op | source)
XLA Modules:
  0.0 98.0 jit_solution(348473740549085914)
XLA Ops:
  0.6 92.6 %shard_map.137 = (bf16[128,2048]{1,0:T(8,128)(2,1)}, f32[3,256,256]{2,1,0:T(8,128)}, f32[11,256]{1,0:T(8,128)}, f32[4,256]{1,0:T(4,128)}, f32[1,256]{1,0:T(1,128)}) custom-call(s32[2,64]{1,0:T(2,128)} %bitcast.10, s32[1,64]{1,0:T(1,128)} %bitcast.13, bf16[128,32,128]{2,1,0:T(8,128)(2,1)} %bitcast.7, bf16[128,2048]{1,0:T(8,128)(2,1)} %den_ref.1, ...), custom_call_target="tpu_custom_call" | custom-call | tf_op jit(solution)/shard_map/pallas_call | solution.py:527
  93.2 0.0 copy-start
  93.2 2.0 %copy.20 = bf16[128,2048]{1,0:T(8,128)(2,1)} copy(bf16[128,2048]{1,0:T(8,128)(2,1)} %get-tuple-element.20) | data formatting | bytes 1048576
  95.2 0.0 copy-done
  95.2 0.0 copy-start.1
  95.2 0.9 copy.21
  96.1 0.0 copy-done.1
  96.1 0.0 copy-start.2
  96.1 0.6 copy.22
  96.7 0.1 copy-done.2
  96.8 0.0 copy-start.3
  96.8 0.6 copy.23
  97.4 0.1 copy-done.3
  97.4 0.6 copy.24
Async XLA Ops:
  93.2 2.0 %copy-start = (f32[3,256,256]{2,1,0:T(8,128)S(1)}, f32[3,256,256]{2,1,0:T(8,128)}, u32[]{:S(2)}) copy-start(f32[3,256,256]{2,1,0:T(8,128)} %get-tuple-element.21) | copy-start | bytes 2359300
  95.2 0.9 copy-start.1
  96.1 0.7 copy-start.2
  96.8 0.7 copy-start.3
